TPU v7x, 256 devices: a whole 4x4x8 slice. The times are simulated.
256 devices in a mesh: cuts: 16 (over x_hi, y, core), row: 16 (over z, x_lo).
Axes of the slice: x: 4 (x_hi: 2, x_lo: 2; x = x_hi * 2 + x_lo), y: 4, z: 8, core: 2. Of those that a mesh axis runs over, the one named last changes fastest.
Arguments:
- vectors: float32 [16, 65536, 192], P('cuts', 'row'), as said below
- images: float32 [16, 65536, 192], P('cuts', 'row'), as said below
- kept_flags: int32 [16, 192], replicated, may hold values from 0 to 1, as said below
Outputs:
- residual: float32 [16, 65536, 192], P('cuts', 'row')
- kept_columns: float32 [16, 65536, 96], P('cuts', 'row')
Inputs may be any that keep to these rules, and one draw needn't show every extreme that they name: `vectors`: no structure is promised. `images`: no structure is promised. `kept_flags`: slices 0 to s together keep between 96 * (s + 1) and 96 * (s + 2) - 1 columns, and all slices together exactly 1536; in every draw, for some s below the last slice, slices 0 to s keep exactly 96 * (s + 2) - 1.
All inputs are finite; a program needn't handle non-finite values.
Results may differ from a plain program's by a relative error of at most 0.0003.
Values sent between devices are 32-bit elements; how exact they have to be, the bound alone decides.
A program may use at most 64 MiB of HBM per device.

v0:
```python
import jax
import jax.numpy as jnp
from jax import lax
from jax.sharding import PartitionSpec as P

SHARED = 64
KEEP_DEV = 96


def passed_along(value, axis, steps):
    count = lax.axis_size(axis)
    first, last = (max(0, -steps), min(count, count - steps))
    return lax.ppermute(value, axis, [(source, source + steps) for source in range(first, last)])


def solve_coeff(gram, projected):
    factor = jnp.linalg.cholesky(gram)
    middle = jax.scipy.linalg.solve_triangular(factor, projected, lower=True)
    return jax.scipy.linalg.solve_triangular(factor, middle, lower=True, trans=1)


def on_device(vectors, images, kept_flags):
    high = lax.Precision.HIGHEST
    width = vectors.shape[2]
    slice_id = lax.axis_index("cuts")
    slice_count = lax.axis_size("cuts")
    head = jnp.concatenate([vectors[:, :, :SHARED], images[:, :, :SHARED]], 2)
    tail = jnp.concatenate([vectors[:, :, width - SHARED :], images[:, :, width - SHARED :]], 2)
    from_lower = passed_along(tail, "cuts", 1)
    from_upper = passed_along(head, "cuts", -1)
    new_head = jnp.where(slice_id > 0, 0.5 * (head + from_lower), head)[0]
    new_tail = jnp.where(slice_id < slice_count - 1, 0.5 * (tail + from_upper), tail)[0]
    basis = jnp.concatenate(
        [new_head[:, :SHARED], vectors[0, :, SHARED : width - SHARED], new_tail[:, :SHARED]], 1
    )
    applied = jnp.concatenate(
        [new_head[:, SHARED:], images[0, :, SHARED : width - SHARED], new_tail[:, SHARED:]], 1
    )
    gram_local = lax.dot_general(
        basis, basis, (((0,), (0,)), ((), ())), precision=high, preferred_element_type=jnp.float32
    )
    projected_local = lax.dot_general(
        basis, applied, (((0,), (0,)), ((), ())), precision=high, preferred_element_type=jnp.float32
    )
    gram, projected = lax.psum((gram_local, projected_local), "row")
    coeff = solve_coeff(gram, projected)
    rotated = jnp.dot(basis, coeff, precision=high, preferred_element_type=jnp.float32)
    residual = (applied - rotated)[None]
    counts = jnp.sum(kept_flags, axis=1)
    slice_ids = jnp.arange(kept_flags.shape[0], dtype=jnp.int32)
    my_offset = jnp.sum(jnp.where(slice_ids < slice_id, counts, 0))
    my_flags = lax.dynamic_slice_in_dim(kept_flags, slice_id, 1, 0)[0]
    ranks = jnp.cumsum(my_flags) - my_flags
    position = my_offset + ranks
    own_slot = position - slice_id * KEEP_DEV
    next_slot = position - (slice_id + 1) * KEEP_DEV
    slots = jnp.arange(KEEP_DEV, dtype=jnp.int32)[None, :]
    chosen = my_flags[:, None] == 1
    select_own = jnp.logical_and(chosen, own_slot[:, None] == slots).astype(jnp.float32)
    select_next = jnp.logical_and(chosen, next_slot[:, None] == slots).astype(jnp.float32)
    selection = jnp.concatenate([select_own, select_next], 1)
    placed = jnp.dot(rotated, selection, precision=high, preferred_element_type=jnp.float32)
    arrived = passed_along(placed[None, :, KEEP_DEV:], "cuts", 1)
    kept_columns = placed[None, :, :KEEP_DEV] + arrived
    return (residual, kept_columns)


def solution(mesh):
    placed = (P("cuts", "row", None), P("cuts", "row", None), P())
    return jax.shard_map(
        on_device,
        mesh=mesh,
        in_specs=placed,
        out_specs=(P("cuts", "row", None), P("cuts", "row", None)),
        check_vma=False,
    )
```

profile of v0, /device:TPU:4, one launch (start us, length us, event | category | flops | bytes accessed | tf_op | source)
XLA Modules:
  0.0 329.9 jit_solution(17466428408134469421)
XLA Ops:
  7.2 4.9 %slice_bitcast_fusion.2 = (f32[4096,64]{0,1:T(8,128)}, f32[1,4096,64]{1,2,0:T(8,128)}, f32[1,4096,64]{1,2,0:T(8,128)S(1)}, f32[1,4096,64]{1,2,0:T(8,128)S(1)}, f...) fusion(f32[1,4096,192]{1,2,0:T(8,128)} %param.3, f32[1,4096,192]{1,2,0:T(8,128)} %param.4), kind=kLoop, calls=%fused_computation.15 | loop fusion | bytes 12582912 | tf_op jit(solution)/shard_map/squeeze | solution.py:34
  12.1 1.5 pad_maximum_fusion.4
  13.6 1.9 collective-permute-start
  15.6 29.2 %collective-permute-done = f32[1,4096,128]{1,2,0:T(8,128)} collective-permute-done((f32[1,4096,128]{1,2,0:T(8,128)}, f32[1,4096,128]{1,2,0:T(8,128)}, u32[]{:S(2)}, u32[]{:S(2)}) %collective-permute-start) | collective-permute-done | bytes 2097184 | tf_op jit(solution)/shard_map/ppermute | solution.py:13
  44.8 4.6 %select_bitcast_fusion.1 = (f32[4096,128]{0,1:T(8,128)}, f32[1,4096,128]{1,2,0:T(8,128)}) fusion(f32[1,4096,128]{1,2,0:T(8,128)} %collective-permute-done, pred[]{:T(512)S(6)} %gt.3, f32[1,4096,64]{1,2,0:T(8,128)} %get-tuple-element.47, f32[1,4096,64]{1,2,0:T(8,128)} %get-tuple-element.28), kind=kLoop, calls=%fused_computation.7 | loop fusion | flops 2097152 | bytes 8388609 | tf_op jit(solution)/shard_map/squeeze | solution.py:31
  49.4 1.9 collective-permute-start.1
  53.2 1.7 fusion.31
  55.0 20.2 %collective-permute-done.1 = f32[1,4096,128]{1,2,0:T(8,128)} collective-permute-done((f32[1,4096,128]{1,2,0:T(8,128)}, f32[1,4096,128]{1,2,0:T(8,128)}, u32[]{:S(2)}, u32[]{:S(2)}) %collective-permute-start.1) | collective-permute-done | bytes 2097184 | tf_op jit(solution)/shard_map/ppermute | solution.py:13
  75.2 1.9 select_bitcast_fusion
  77.3 1.4 copy-done
  78.7 3.4 %fusion.3 = f32[192,192]{0,1:T(8,128)} fusion(f32[4096,64]{0,1:T(8,128)S(1)} %get-tuple-element.33, f32[4096,64]{0,1:T(8,128)S(1)} %copy-done, f32[4096,64]{0,1:T(8,128)S(1)} %get-tuple-element.31), kind=kOutput, calls=%fused_computation.12 | convolution fusion | flops 1813512192 | bytes 3293184 | tf_op jit(solution)/shard_map/dot_general | solution.py:39
  82.0 3.4 %fusion = f32[192,192]{1,0:T(8,128)} fusion(f32[4096,64]{0,1:T(8,128)S(1)} %get-tuple-element.32, f32[4096,64]{0,1:T(8,128)S(1)} %get-tuple-element.48, f32[4096,64]{0,1:T(8,128)S(1)} %get-tuple-element.30, f32[4096,64]{0,1:T(8,128)S(1)} %get-tuple-element.33, f32[4096,64]{0,1:T(8,128)S(1)} %copy-done, f32[4096,64]{0,1:T(8,128)S(1)} %get-tuple-element.31), kind=kOutput, calls=%fused_computation.3 | convolution fusion | flops 1815085056 | bytes 6438912 | tf_op jit(solution)/shard_map/dot_general | solution.py:42
  86.1 0.8 fusion.14
  86.8 138.4 %all-reduce.7.cloned.1.call-done = (f32[192,192]{1,0:T(8,128)}, f32[192,192]{0,1:T(8,128)}) async-done(((f32[192,192]{1,0:T(8,128)}, f32[192,192]{0,1:T(8,128)}), (f32[192,192]{1,0:T(8,128)}, f32[192,192]{0,1:T(8,128)})) %all-reduce.7.cloned.1.call-update) | async-done | bytes 294928 | tf_op jit(solution)/shard_map/psum | solution.py:45
  225.2 1.0 copy.8
  226.3 1.0 fusion.7
  227.2 11.7 %cholesky.51 = f32[128,128]{1,0:T(8,128)S(1)} custom-call(f32[128,128]{1,0:T(8,128)S(1)} %cholesky.124), custom_call_target="Cholesky" | custom-call | tf_op jit(solution)/shard_map/jit(cholesky)/cholesky | solution.py:17
  240.2 0.9 cholesky.119
  241.1 11.4 %custom-call.18 = f32[1,128,128]{1,2,0:T(8,128)} custom-call(f32[1,128,128]{2,1,0:T(8,128)} %get-tuple-element.37), custom_call_target="InvertDiagBlocksLowerTriangular" | custom-call | tf_op jit(solution)/shard_map/jit(cholesky)/cholesky | solution.py:17
  252.5 1.0 constant_dynamic-update-slice_fusion.1
  253.5 0.8 convolution_subtract_fusion.1
  254.3 6.6 %cholesky.110 = f32[64,64]{1,0:T(8,128)S(1)} custom-call(f32[64,64]{1,0:T(8,128)} %convolution_subtract_fusion.1), custom_call_target="Cholesky" | custom-call | tf_op jit(solution)/shard_map/jit(cholesky)/cholesky | solution.py:17
  263.6 0.9 fusion.17
  265.2 20.5 %custom-call.19 = f32[2,128,128]{1,2,0:T(8,128)S(1)} custom-call(f32[2,128,128]{2,1,0:T(8,128)} %pad_maximum_fusion.8), custom_call_target="InvertDiagBlocksLowerTriangular" | custom-call | tf_op jit(solution)/shard_map/jit(_solve_triangular)/triangular_solve | solution.py:19
  285.7 1.3 fusion.12
  287.3 1.1 fusion.16
  289.4 4.7 %fusion.2 = f32[4096,192]{0,1:T(8,128)S(1)} fusion(f32[4096,64]{0,1:T(8,128)} %copy-done.4, f32[4096,64]{0,1:T(8,128)S(1)} %copy-done, f32[4096,64]{0,1:T(8,128)} %copy-done.3, f32[64,192]{1,0:T(8,128)S(1)} %fusion.22, f32[128,192]{1,0:T(8,128)S(1)} %fusion.20), kind=kOutput, calls=%fused_computation.11 | convolution fusion | flops 1813549056 | bytes 6438912 | tf_op jit(solution)/shard_map/dot_general | solution.py:47
  294.1 2.0 fusion.8
  296.2 2.1 collective-permute-start.2
  298.3 2.1 subtract_bitcast_fusion
  300.4 21.3 %collective-permute-done.2 = f32[1,4096,96]{1,2,0:T(8,128)S(1)} collective-permute-done((f32[1,4096,96]{1,2,0:T(8,128)S(1)}, f32[1,4096,96]{1,2,0:T(8,128)S(1)}, u32[]{:S(2)}, u32[]{:S(2)}) %collective-permute-start.2) | collective-permute-done | bytes 1572896 | tf_op jit(solution)/shard_map/ppermute | solution.py:13
  321.7 1.3 fusion.1
  (47 shorter events, 7.5 us)
Async XLA Ops:
  7.2 218.1 %all-reduce.7.cloned.1.call-start = ((), (), s32[]{:S(2)}) async-start(), calls=%async_computation | async-start | bytes 786432 | tf_op jit(solution)/shard_map/psum | solution.py:45
  12.1 3.4 %copy-start.8 = (s32[16,192]{1,0:T(8,128)S(1)}, s32[16,192]{1,0:T(8,128)}, u32[]{:S(2)}) copy-start(s32[16,192]{1,0:T(8,128)} %param.5) | copy-start | bytes 36868
  13.6 31.3 %collective-permute-start = (f32[1,4096,128]{1,2,0:T(8,128)}, f32[1,4096,128]{1,2,0:T(8,128)}, u32[]{:S(2)}, u32[]{:S(2)}) collective-permute-start(f32[1,4096,128]{1,2,0:T(8,128)} %pad_maximum_fusion.4), channel_id=1, source_target_pairs={{0,16},{16,32},{32,48},{48,64},{64,80},{80,96},{96,112},{112,128},... | collective-permute-start | bytes 6291464 | tf_op jit(solution)/shard_map/ppermute | solution.py:13
  49.4 25.8 %collective-permute-start.1 = (f32[1,4096,128]{1,2,0:T(8,128)}, f32[1,4096,128]{1,2,0:T(8,128)}, u32[]{:S(2)}, u32[]{:S(2)}) collective-permute-start(f32[1,4096,128]{1,2,0:T(8,128)} %get-tuple-element.35), channel_id=1, source_target_pairs={{16,0},{32,16},{48,32},{64,48},{80,64},{96,80},{112,96},{128,112},... | collective-permute-start | bytes 6291464 | tf_op jit(solution)/shard_map/ppermute | solution.py:13
  54.9 27.1 %copy-start.1 = (f32[4096,64]{0,1:T(8,128)}, f32[4096,64]{0,1:T(8,128)S(1)}, u32[]{:S(2)}) copy-start(f32[4096,64]{0,1:T(8,128)S(1)} %get-tuple-element.30) | copy-start | bytes 3145732
  55.0 27.1 %copy-start.3 = (f32[4096,64]{0,1:T(8,128)}, f32[4096,64]{0,1:T(8,128)S(1)}, u32[]{:S(2)}) copy-start(f32[4096,64]{0,1:T(8,128)S(1)} %get-tuple-element.31) | copy-start | bytes 3145732
  77.1 1.6 copy-start
  77.3 4.8 %copy-start.4 = (f32[4096,64]{0,1:T(8,128)}, f32[4096,64]{0,1:T(8,128)S(1)}, u32[]{:S(2)}) copy-start(f32[4096,64]{0,1:T(8,128)S(1)} %get-tuple-element.33) | copy-start | bytes 3145732
  239.0 0.6 copy-start.5
  289.3 4.7 %copy-start.6 = (pred[192,96]{1,0:T(32,128)(4,1)S(1)}, pred[192,96]{1,0:T(32,128)(4,1)}, u32[]{:S(2)}) copy-start(pred[192,96]{1,0:T(32,128)(4,1)} %get-tuple-element.42) | copy-start | bytes 55300
  289.4 4.7 %copy-start.7 = (pred[192,96]{1,0:T(32,128)(4,1)S(1)}, pred[192,96]{1,0:T(32,128)(4,1)}, u32[]{:S(2)}) copy-start(pred[192,96]{1,0:T(32,128)(4,1)} %get-tuple-element.43) | copy-start | bytes 55300
  296.1 2.2 copy-start.2
  296.2 25.5 %collective-permute-start.2 = (f32[1,4096,96]{1,2,0:T(8,128)S(1)}, f32[1,4096,96]{1,2,0:T(8,128)S(1)}, u32[]{:S(2)}, u32[]{:S(2)}) collective-permute-start(f32[1,4096,96]{1,2,0:T(8,128)S(1)} %slice_bitcast_fusion), channel_id=1, source_target_pairs={{0,16},{16,32},{32,48},{48,64},{64,80},{80,96},{96,112},{112,128},... | collective-permute-start | bytes 4718600 | tf_op jit(solution)/shard_map/ppermute | solution.py:13
Sparse Core Ops, SparseCore 0:
  85.6 139.6 all-reduce.6
where the time goes:
time: 331 us; the launch traced here: 330 us
  waiting for transfers between devices  209 us (63%)
  other arithmetic  69.4 us (21%)
  matrix products  18.8 us (6%)
  between operations  15.6 us (5%)
  local copies, waits for them, and re-layouts  11 us (3%)
  starting transfers between devices  5.91 us (2%)
    psum x1, waiting for transfers between devices, on_device(): gram, projected = lax.psum((gram_local, projected_local), 'row')  138 us
    ppermute x3, waiting for transfers between devices, passed_along(): lax.ppermute(value, axis, [(source, source + steps) for source in range(f...  70.8 us
    another operation x7, other arithmetic, solve_coeff(): factor = jnp.linalg.cholesky(gram)  31.7 us
    another operation x6, other arithmetic, solve_coeff(): jax.scipy.linalg.solve_triangular(factor, middle, lower=True, trans=1)  22.7 us
  transfers between devices with their start and end apart: 4, of which 4 were waited for; matrix products, arithmetic and copies ran while one was open for 2% of the time, Pallas kernels for 0%

commit v1 on v0

v1 whole, which is shorter than its diff:
```python
import functools

import jax
import jax.numpy as jnp
from jax import lax
from jax.experimental import pallas as pl
from jax.experimental.pallas import tpu as pltpu
from jax.sharding import PartitionSpec as P

W = 192
SHARED = 64
KEEP_DEV = 96
SLICES = 16
ROWS = 4096
PEERS = 16
CHUNKS = 4
CHUNK = ROWS // CHUNKS
LANES = 256
PACK_G = 256
PACK_P = 384
F32 = jnp.float32
HIGH = lax.Precision.HIGHEST
MESH = pl.DeviceIdType.MESH
ANY = pl.BlockSpec(memory_space=pl.ANY)
VMEM = pl.BlockSpec(memory_space=pltpu.VMEM)


def dot_rows(a, b):
    return lax.dot_general(a, b, (((1,), (1,)), ((), ())), precision=HIGH, preferred_element_type=F32)


def dot(a, b):
    return lax.dot_general(a, b, (((1,), (0,)), ((), ())), precision=HIGH, preferred_element_type=F32)


def sweep_block(kb, a_ref, d_ref):
    base = pl.multiple_of(kb * 8, 8)
    lane = lax.broadcasted_iota(jnp.int32, (8, LANES), 1) - base
    in_block = jnp.logical_and(lane >= 0, lane < 8)
    diag = a_ref[pl.ds(base, 8), pl.ds(pl.multiple_of((kb // 16) * 128, 128), 128)]
    diag = pltpu.roll(diag, lax.rem(128 - lax.rem(base, 128), 128), 1)
    for j in range(8):
        d_ref[j] = jnp.broadcast_to(diag[:, j : j + 1], (8, 128))
    d = {}
    for i in range(8):
        for j in range(i, 8):
            d[i, j] = jnp.broadcast_to(d_ref[j, i : i + 1, :], (8, 128))

    def at(i, j):
        return d[min(i, j), max(i, j)]

    for k in range(8):
        pivot = 1.0 / d[k, k]
        scaled = {i: at(i, k) * pivot for i in range(8) if i != k}
        for i in range(8):
            for j in range(i, 8):
                if i != k and j != k:
                    d[i, j] = d[i, j] - scaled[i] * at(j, k)
        for i in range(8):
            if i != k:
                d[min(i, k), max(i, k)] = scaled[i]
        d[k, k] = -pivot
    rows = []
    for j in range(8):
        row = jnp.broadcast_to(a_ref[pl.ds(base + j, 1), :], (8, LANES))
        rows.append(jnp.where(in_block, jnp.where(lane == j, 1.0, 0.0), -row))
    solved = []
    for i in range(8):
        total = None
        for j in range(8):
            term = jnp.concatenate([at(i, j)] * 2, 1) * rows[j]
            total = term if total is None else total + term
        solved.append(total)
    columns = a_ref[pl.ds(base, 8), :].T
    for t in range(W // 8):
        total = jnp.where(in_block, 0.0, a_ref[8 * t : 8 * t + 8, :])
        for j in range(8):
            total = total - jnp.broadcast_to(columns[8 * t : 8 * t + 8, j : j + 1], (8, LANES)) * solved[j]
        a_ref[8 * t : 8 * t + 8, :] = total
    sublane = lax.broadcasted_iota(jnp.int32, (8, LANES), 0)
    mine = solved[0]
    for i in range(1, 8):
        mine = jnp.where(sublane == i, solved[i], mine)
    a_ref[pl.ds(base, 8), :] = mine


def solve_kernel(
    v_hbm, i_hbm, flags_ref,
    x_out, y_out, xp_out, c_ref, kp_ref,
    x, y, tv, hv, ti, hi, gram, proj, gpack, gparts, gfull, ppack, pparts, pfull, mine_g, mine_p,
    a_ref, d_ref, kn, kp,
    load_sem, ex_send, ex_recv, sum_send, sum_recv, fwd_send, fwd_recv, out_sem,
):
    s = lax.axis_index("cuts")
    r = lax.axis_index("row")
    has_lower = s > 0
    has_upper = s < SLICES - 1
    upper = lax.rem(s + 1, SLICES)
    lower = lax.rem(s + SLICES - 1, SLICES)

    load_x = pltpu.make_async_copy(v_hbm, x, load_sem.at[0])
    load_y = pltpu.make_async_copy(i_hbm, y, load_sem.at[1])
    load_x.start()
    load_y.start()

    barrier = pltpu.get_barrier_semaphore()
    for q in (lower, upper):
        pl.semaphore_signal(barrier, inc=1, device_id=(q, r), device_id_type=MESH)

    def greet(i, carry):
        pl.semaphore_signal(barrier, inc=1, device_id=(s, lax.rem(r + i, PEERS)), device_id_type=MESH)
        return carry

    lax.fori_loop(1, PEERS, greet, 0)
    pl.semaphore_wait(barrier, PEERS + 1)

    def lanes(c):
        return pl.ds(pl.multiple_of(c * CHUNK, CHUNK), CHUNK)

    def exchange(kind, c, up):
        src = (v_hbm, i_hbm)[kind]
        dst = ((tv, ti), (hv, hi))[0 if up else 1][kind]
        first = W - SHARED if up else 0
        way = 0 if up else 1
        return pltpu.make_async_remote_copy(
            src_ref=src.at[pl.ds(first, SHARED), lanes(c)],
            dst_ref=dst.at[:, lanes(c)],
            send_sem=ex_send.at[kind, way, c],
            recv_sem=ex_recv.at[kind, way, c],
            device_id=(upper if up else lower, r),
            device_id_type=MESH,
        )

    def send(kind, c):
        @pl.when(has_upper)
        def _():
            exchange(kind, c, True).start()

        @pl.when(has_lower)
        def _():
            exchange(kind, c, False).start()

    def receive(kind, c):
        @pl.when(has_lower)
        def _():
            exchange(kind, c, True).wait_recv()

        @pl.when(has_upper)
        def _():
            exchange(kind, c, False).wait_recv()

    def blend(own, low, high, c):
        head = own[0:SHARED, lanes(c)]
        tail = own[W - SHARED : W, lanes(c)]
        own[0:SHARED, lanes(c)] = jnp.where(has_lower, 0.5 * (head + low[:, lanes(c)]), head)
        own[W - SHARED : W, lanes(c)] = jnp.where(has_upper, 0.5 * (tail + high[:, lanes(c)]), tail)

    for c in range(CHUNKS):
        send(0, c)
    load_x.wait()
    gram[...] = jnp.zeros_like(gram)
    proj[...] = jnp.zeros_like(proj)

    def gram_step(c, carry):
        receive(0, c)
        blend(x, tv, hv, c)
        part = x[:, lanes(c)]
        gram[...] += dot_rows(part, part)

        @pl.when(c == CHUNKS - 2)
        def _():
            send(1, 0)

        return carry

    lax.fori_loop(0, CHUNKS, gram_step, 0)
    for c in range(1, CHUNKS):
        send(1, c)

    def scatter(which, pack, parts, chunk):
        def one(i, carry):
            q = lax.rem(r + i, PEERS)
            pltpu.make_async_remote_copy(
                src_ref=pack.at[pl.ds(pl.multiple_of(q * chunk, 8), chunk), :],
                dst_ref=parts.at[i - 1],
                send_sem=sum_send.at[which],
                recv_sem=sum_recv.at[which],
                device_id=(s, q),
                device_id_type=MESH,
            ).start()
            return carry

        lax.fori_loop(1, PEERS, one, 0)

    def all_parts(which, parts):
        return pltpu.make_async_remote_copy(
            src_ref=parts,
            dst_ref=parts,
            send_sem=sum_send.at[which],
            recv_sem=sum_recv.at[which],
            device_id=(s, lax.rem(r + 1, PEERS)),
            device_id_type=MESH,
        )

    def add_parts(pack, parts, mine, full, chunk):
        place = pl.ds(pl.multiple_of(r * chunk, 8), chunk)
        total = pack[place, :]
        for i in range(PEERS - 1):
            total = total + parts[i]
        mine[...] = total
        full[place, :] = total

    def gather(which, mine, full, chunk):
        place = pl.ds(pl.multiple_of(r * chunk, 8), chunk)

        def one(i, carry):
            pltpu.make_async_remote_copy(
                src_ref=mine,
                dst_ref=full.at[place, :],
                send_sem=sum_send.at[which],
                recv_sem=sum_recv.at[which],
                device_id=(s, lax.rem(r + i, PEERS)),
                device_id_type=MESH,
            ).start()
            return carry

        lax.fori_loop(1, PEERS, one, 0)

    gpack[0:W, :] = gram[:, 0:128]
    gpack[W:PACK_G, 0:64] = gram[128:W, 128:W]
    gpack[W:PACK_G, 64:128] = jnp.zeros((64, 64), F32)
    scatter(0, gpack, gparts, PACK_G // PEERS)

    load_y.wait()

    def proj_step(c, carry):
        receive(1, c)
        blend(y, ti, hi, c)
        proj[...] += dot_rows(y[:, lanes(c)], x[:, lanes(c)])
        return carry

    lax.fori_loop(0, 1, proj_step, 0)

    all_parts(0, gparts).wait_recv()
    add_parts(gpack, gparts, mine_g, gfull, PACK_G // PEERS)
    gather(1, mine_g, gfull, PACK_G // PEERS)

    lax.fori_loop(1, CHUNKS, proj_step, 0)

    def forward(k):
        src = x.at[0:SHARED, :] if k == 0 else v_hbm.at[SHARED : 2 * SHARED, :]
        return pltpu.make_async_remote_copy(
            src_ref=src,
            dst_ref=xp_out.at[pl.ds(k * SHARED, SHARED), :],
            send_sem=fwd_send.at[k],
            recv_sem=fwd_recv.at[k],
            device_id=(upper, r),
            device_id_type=MESH,
        )

    save_x = pltpu.make_async_copy(x, x_out, out_sem.at[0])
    save_y = pltpu.make_async_copy(y, y_out, out_sem.at[1])
    fill = pltpu.make_async_copy(x.at[0:128, :], xp_out, out_sem.at[2])

    @pl.when(has_upper)
    def _():
        forward(1).start()
        forward(0).start()

    save_x.start()
    save_y.start()

    @pl.when(jnp.logical_not(has_lower))
    def _():
        fill.start()

    ppack[0:W, :] = proj[:, 0:128]
    ppack[W : 2 * W, 0:64] = proj[:, 128:W]
    ppack[W : 2 * W, 64:128] = jnp.zeros((W, 64), F32)
    scatter(2, ppack, pparts, PACK_P // PEERS)

    all_parts(1, gparts).wait_recv()
    a_ref[:, 0:128] = gfull[0:W, :]
    corner = jnp.concatenate([gfull[128:W, :].T, gfull[W:PACK_G, 0:64]], 0)
    a_ref[:, 128:LANES] = jnp.concatenate([corner, jnp.zeros((W, 64), F32)], 1)

    def sweep_step(kb, carry):
        sweep_block(kb, a_ref, d_ref)
        return carry

    lax.fori_loop(0, 12, sweep_step, 0)
    all_parts(2, pparts).wait_recv()
    add_parts(ppack, pparts, mine_p, pfull, PACK_P // PEERS)
    gather(3, mine_p, pfull, PACK_P // PEERS)
    lax.fori_loop(12, 24, sweep_step, 0)

    flags = flags_ref[...].astype(F32)
    row_id = lax.broadcasted_iota(jnp.int32, (SLICES, W), 0)
    before = jnp.sum(jnp.where(row_id < s, flags, 0.0), keepdims=True)
    own_flags = jnp.sum(jnp.where(row_id == s, flags, 0.0), axis=0, keepdims=True)
    earlier = lax.broadcasted_iota(jnp.int32, (W, W), 0) < lax.broadcasted_iota(jnp.int32, (W, W), 1)
    ranks = dot(jnp.broadcast_to(own_flags, (8, W)), jnp.where(earlier, 1.0, 0.0))[0:1]
    slot = ranks + before - (s * KEEP_DEV).astype(F32)
    slot_id = lax.broadcasted_iota(jnp.int32, (W, W), 0).astype(F32)
    select = jnp.where(jnp.logical_and(slot_id == slot, own_flags > 0.5), 1.0, 0.0)

    all_parts(3, pparts).wait_recv()
    proj_sum = jnp.concatenate([pfull[0:W, :], pfull[W : 2 * W, 0:64]], 1)
    coeff = dot(proj_sum, -a_ref[:, 0:W])
    placed = dot(select, coeff)
    kn[...] = placed[KEEP_DEV:W]

    late = pltpu.make_async_remote_copy(
        src_ref=kn,
        dst_ref=kp,
        send_sem=fwd_send.at[2],
        recv_sem=fwd_recv.at[2],
        device_id=(upper, r),
        device_id_type=MESH,
    )

    @pl.when(has_upper)
    def _():
        late.start()

    c_ref[0:W, :] = coeff

    for kind in range(2):
        for c in range(CHUNKS):

            @pl.when(has_upper)
            def _():
                exchange(kind, c, True).wait_send()

            @pl.when(has_lower)
            def _():
                exchange(kind, c, False).wait_send()

    all_parts(0, gparts).wait_send()
    all_parts(1, gparts).wait_send()
    all_parts(2, pparts).wait_send()
    all_parts(3, pparts).wait_send()
    save_x.wait()
    save_y.wait()

    @pl.when(jnp.logical_not(has_lower))
    def _():
        fill.wait()
        kp[...] = jnp.zeros_like(kp)

    @pl.when(has_lower)
    def _():
        forward(1).wait_recv()
        forward(0).wait_recv()
        late.wait_recv()

    previous = kp[...]
    shift = jnp.concatenate([previous[:, 128:W], jnp.zeros((KEEP_DEV, 128), F32)], 1)
    c_ref[W : W + KEEP_DEV, :] = placed[0:KEEP_DEV] + shift
    kp_ref[...] = previous[:, 0:128]

    @pl.when(has_upper)
    def _():
        forward(1).wait_send()
        forward(0).wait_send()
        late.wait_send()


def solve_call(vectors, images, flags):
    shape = jax.ShapeDtypeStruct
    big = pltpu.VMEM((W, ROWS), F32)
    shared = pltpu.VMEM((SHARED, ROWS), F32)
    dma = pltpu.SemaphoreType.DMA
    chunk_g, chunk_p = PACK_G // PEERS, PACK_P // PEERS
    return pl.pallas_call(
        solve_kernel,
        out_shape=(
            shape((W, ROWS), F32), shape((W, ROWS), F32), shape((2 * SHARED, ROWS), F32),
            shape((W + KEEP_DEV, W), F32), shape((KEEP_DEV, 2 * SHARED), F32),
        ),
        in_specs=[ANY, ANY, VMEM],
        out_specs=(ANY, ANY, ANY, VMEM, VMEM),
        scratch_shapes=[
            big, big, shared, shared, shared, shared,
            pltpu.VMEM((W, W), F32), pltpu.VMEM((W, W), F32),
            pltpu.VMEM((PACK_G, 128), F32), pltpu.VMEM((PEERS - 1, chunk_g, 128), F32), pltpu.VMEM((PACK_G, 128), F32),
            pltpu.VMEM((PACK_P, 128), F32), pltpu.VMEM((PEERS - 1, chunk_p, 128), F32), pltpu.VMEM((PACK_P, 128), F32),
            pltpu.VMEM((chunk_g, 128), F32), pltpu.VMEM((chunk_p, 128), F32),
            pltpu.VMEM((W, LANES), F32), pltpu.VMEM((8, 8, 128), F32),
            pltpu.VMEM((KEEP_DEV, W), F32), pltpu.VMEM((KEEP_DEV, W), F32),
            dma((2,)), dma((2, 2, CHUNKS)), dma((2, 2, CHUNKS)), dma((4,)), dma((4,)), dma((3,)), dma((3,)), dma((3,)),
        ],
        compiler_params=pltpu.CompilerParams(
            collective_id=0, has_side_effects=True, vmem_limit_bytes=40 << 20
        ),
        name="exchange_and_solve",
    )(vectors, images, flags)


def rotate_kernel(x_ref, y_ref, xp_ref, c_ref, kp_ref, res_ref, kept_ref):
    both = dot(c_ref[...], x_ref[...])
    res_ref[...] = y_ref[...] - both[0:W]
    kept_ref[...] = both[W : W + KEEP_DEV] + dot(kp_ref[...], xp_ref[...])


def rotate_call(x, y, xp, c, kp):
    block = 512

    def tall(rows):
        return pl.BlockSpec((rows, block), lambda i: (0, i))

    def whole(shape):
        return pl.BlockSpec(shape, lambda i: (0, 0))

    return pl.pallas_call(
        rotate_kernel,
        grid=(ROWS // block,),
        out_shape=(jax.ShapeDtypeStruct((W, ROWS), F32), jax.ShapeDtypeStruct((KEEP_DEV, ROWS), F32)),
        in_specs=[tall(W), tall(W), tall(2 * SHARED), whole((W + KEEP_DEV, W)), whole((KEEP_DEV, 2 * SHARED))],
        out_specs=(tall(W), tall(KEEP_DEV)),
        compiler_params=pltpu.CompilerParams(vmem_limit_bytes=40 << 20),
        name="rotate",
    )(x, y, xp, c, kp)


def on_device(vectors, images, kept_flags):
    x, y, xp, c, kp = solve_call(vectors[0].T, images[0].T, kept_flags)
    residual, kept = rotate_call(x, y, xp, c, kp)
    return residual.T[None], kept.T[None]


def solution(mesh):
    placed = (P("cuts", "row", None), P("cuts", "row", None), P())
    return jax.shard_map(
        on_device,
        mesh=mesh,
        in_specs=placed,
        out_specs=(P("cuts", "row", None), P("cuts", "row", None)),
        check_vma=False,
    )
```

time: 331 us -> 90.6 us (0.27)
  waiting for transfers between devices: 209 us -> 0 us
  Pallas kernels: 0 us -> 87 us
  other arithmetic: 69.4 us -> 0 us
  matrix products: 18.8 us -> 0 us
  between operations: 15.6 us -> 0.65 us
  local copies, waits for them, and re-layouts: 11 us -> 2.6 us
  starting transfers between devices: 5.91 us -> 0 us
    psum x1 -> x0, waiting for transfers between devices: 138 us -> none  [on_device(): gram, projected = lax.psum((gram_local, projected_local), 'row')]
    pallas_call x0 -> x2, Pallas kernels: none -> 87 us  [the longest x1 79.2 us: solve_call(): pl.pallas_call(solve_kernel, out_shape=(shape((W, ROWS), F32), shape((W,...]
    ppermute x3 -> x0, waiting for transfers between devices: 70.8 us -> none  [passed_along(): lax.ppermute(value, axis, [(source, source + steps) for source in range(f...]
    another operation x16 -> x0, other arithmetic: 54.9 us -> none  [the longest x7 31.7 us: solve_coeff(): factor = jnp.linalg.cholesky(gram)]
    dot_general x4 -> x0, matrix products: 13.4 us -> none  [the longest x1 4.69 us: on_device(): jnp.dot(basis, coeff, precision=high, preferred_element_type=jnp.float32)]
    squeeze x2 -> x0, other arithmetic: 6.48 us -> none  [the longest x1 4.57 us: on_device(): new_head = jnp.where(slice_id > 0, 0.5 * (head + from_lower), head)[0]]
    ppermute x3 -> x0, starting transfers between devices: 5.87 us -> none  [passed_along(): lax.ppermute(value, axis, [(source, source + steps) for source in range(f...]
    another operation x8 -> x0, matrix products: 5.39 us -> none  [the longest x3 2.69 us: solve_coeff(): middle = jax.scipy.linalg.solve_triangular(factor, projected, lower=True)]
  transfers between devices with their start and end apart: 4 -> 0, of which waited for: 4 -> 0; matrix products, arithmetic and copies ran while one was open for 2% -> 0% of each run, Pallas kernels for 0% -> 0%
where the time goes in v1:
time: 90.6 us; the launch traced here: 90.2 us
  Pallas kernels  87 us (96%)
  local copies, waits for them, and re-layouts  2.6 us (3%)
    pallas_call x1, Pallas kernels, solve_call(): pl.pallas_call(solve_kernel, out_shape=(shape((W, ROWS), F32), shape((W,...  79.2 us
    pallas_call x1, Pallas kernels, rotate_call(): pl.pallas_call(rotate_kernel, grid=(ROWS // block,), out_shape=(jax.Shape...  7.75 us
    unnamed x4, local copies, waits for them, and re-layouts  2.6 us

profile of v1, /device:TPU:4, one launch (start us, length us, event | category | flops | bytes accessed | tf_op | source)
XLA Modules:
  0.0 90.2 jit_solution(6322009396531052111)
XLA Ops:
  0.6 0.0 copy-start
  0.6 1.9 %copy-done = f32[1,4096,192]{1,2,0:T(8,128)S(1)} copy-done((f32[1,4096,192]{1,2,0:T(8,128)S(1)}, f32[1,4096,192]{1,2,0:T(8,128)}, u32[]{:S(2)}) %copy-start) | copy-done | bytes 3145752
  2.5 0.0 copy-start.1
  2.5 0.7 copy-done.1
  3.2 79.2 %exchange_and_solve.1 = (f32[192,4096]{1,0:T(8,128)S(1)}, f32[192,4096]{1,0:T(8,128)S(1)}, f32[128,4096]{1,0:T(8,128)S(1)}, f32[288,192]{1,0:T(8,128)S(1)}, f32[96,128]{1,0:T(8,128)S(1)}) custom-call(f32[192,4096]{1,0:T(8,128)S(1)} %bitcast.12, f32[192,4096]{1,0:T(8,128)} %bitcast.13, s32[16,192]{1,0:T(8,128)S(1)} %copy-done.1), custom_call_target="tpu_custom_call" | custom-call | tf_op jit(solution)/shard_map/exchange_and_solve/pallas_call | solution.py:375
  82.5 7.7 %rotate.1 = (f32[192,4096]{1,0:T(8,128)}, f32[96,4096]{1,0:T(8,128)}) custom-call(f32[192,4096]{1,0:T(8,128)S(1)} %get-tuple-element.9.x_ref, f32[192,4096]{1,0:T(8,128)S(1)} %get-tuple-element.10.y_ref, f32[128,4096]{1,0:T(8,128)S(1)} %get-tuple-element.11.xp_ref, f32[288,192]{1,0:T(8,128)S(1)} %get-tuple-element.12.c_ref, ...), custom_call_target="tpu_custom_call" | custom-call | tf_op jit(solution)/shard_map/rotate/pallas_call | solution.py:415
Async XLA Ops:
  0.6 1.9 %copy-start = (f32[1,4096,192]{1,2,0:T(8,128)S(1)}, f32[1,4096,192]{1,2,0:T(8,128)}, u32[]{:S(2)}) copy-start(f32[1,4096,192]{1,2,0:T(8,128)} %param.3) | copy-start | bytes 9437188
  2.5 0.7 copy-start.1

commit v2 on v0

v2 whole, which is shorter than its diff:
```python
import functools

import jax
import jax.numpy as jnp
from jax import lax
from jax.experimental import pallas as pl
from jax.experimental.pallas import tpu as pltpu
from jax.sharding import PartitionSpec as P

W = 192
SHARED = 64
KEEP_DEV = 96
SLICES = 16
ROWS = 4096
PEERS = 16
CHUNKS = 4
CHUNK = ROWS // CHUNKS
EARLY = 2
EARLY_ROWS = EARLY * CHUNK
LANES = 256
PANEL = 48
VMEM_LIMIT = 48 << 20
PACK = (256, 256, 128)
F32 = jnp.float32
BF16 = jnp.bfloat16
HIGH = lax.Precision.HIGHEST
MESH = pl.DeviceIdType.MESH
HBM = pl.BlockSpec(memory_space=pltpu.HBM)
VMEM = pl.BlockSpec(memory_space=pltpu.VMEM)


def split(a):
    high = a.astype(BF16)
    return high, (a - high.astype(F32)).astype(BF16)


def dot_rows(a, b):
    return lax.dot_general(a, b, (((1,), (1,)), ((), ())), preferred_element_type=F32)


def dot_split(a, b):
    def one(x, y):
        return lax.dot_general(x, y, (((1,), (0,)), ((), ())), preferred_element_type=F32)

    return one(a[0], b[0]) + (one(a[0], b[1]) + one(a[1], b[0]))


def dot(a, b):
    return lax.dot_general(a, b, (((1,), (0,)), ((), ())), precision=HIGH, preferred_element_type=F32)


def sweep_block(kb, q, p_ref, d_ref):
    base = kb * 8
    first = 8 * q
    lane = lax.broadcasted_iota(jnp.int32, (8, LANES), 1) - base
    in_block = jnp.logical_and(lane >= 0, lane < 8)
    half = pl.ds(pl.multiple_of((kb // 16) * 128, 128), 128)
    turn = lax.rem(128 - lax.rem(base, 128), 128)
    pivots = {z: pltpu.roll(p_ref[8 * z : 8 * z + 8, half], turn, 1) for z in range(PANEL // 8)}
    for j in range(8):
        d_ref[j] = jnp.broadcast_to(pivots[q][:, j : j + 1], (8, 128))
    d = {}
    for i in range(8):
        for j in range(i, 8):
            d[i, j] = jnp.broadcast_to(d_ref[j, i : i + 1, :], (8, 128))

    def at(i, j):
        return d[min(i, j), max(i, j)]

    for k in range(8):
        pivot = 1.0 / d[k, k]
        scaled = {i: at(i, k) * pivot for i in range(8) if i != k}
        for i in range(8):
            for j in range(i, 8):
                if i != k and j != k:
                    d[i, j] = d[i, j] - scaled[i] * at(j, k)
        for i in range(8):
            if i != k:
                d[min(i, k), max(i, k)] = scaled[i]
        d[k, k] = -pivot
    rows = []
    for j in range(8):
        row = jnp.broadcast_to(p_ref[first + j : first + j + 1, :], (8, LANES))
        rows.append(jnp.where(in_block, jnp.where(lane == j, 1.0, 0.0), -row))
    solved = []
    for i in range(8):
        total = None
        for j in range(8):
            term = jnp.concatenate([at(i, j)] * 2, 1) * rows[j]
            total = term if total is None else total + term
        solved.append(total)
    for z in range(PANEL // 8):
        if z != q:
            total = jnp.where(in_block, 0.0, p_ref[8 * z : 8 * z + 8, :])
            for j in range(8):
                total = total - jnp.broadcast_to(pivots[z][:, j : j + 1], (8, LANES)) * solved[j]
            p_ref[8 * z : 8 * z + 8, :] = total
    sublane = lax.broadcasted_iota(jnp.int32, (8, LANES), 0)
    mine = solved[0]
    for i in range(1, 8):
        mine = jnp.where(sublane == i, solved[i], mine)
    p_ref[first : first + 8, :] = mine


def sweep_panel(step, a_ref, p_ref, d_ref):
    base = pl.multiple_of(step * PANEL, PANEL)
    panel = a_ref[pl.ds(base, PANEL), :]
    p_ref[...] = panel
    for q in range(PANEL // 8):
        sweep_block(step * (PANEL // 8) + q, q, p_ref, d_ref)
    swept = p_ref[...]
    update = lax.dot_general(
        panel[:, 0:W], swept, (((0,), (0,)), ((), ())), precision=HIGH, preferred_element_type=F32
    )
    lane = lax.broadcasted_iota(jnp.int32, (W, LANES), 1) - base
    a_ref[...] = jnp.where(jnp.logical_and(lane >= 0, lane < PANEL), 0.0, a_ref[...]) - update
    a_ref[pl.ds(base, PANEL), :] = swept


def fused_kernel(
    v_hbm, i_hbm, flags_ref,
    res_ref, kept_ref,
    x, y, xh, xl, fv, fi, sv, si, xp, z_out, z_in, g_hh, g_hl, proj,
    pack_g, pack_f, pack_s, parts_g, parts_f, parts_s, mine_g, mine_f, mine_s, full_g, full_f, full_s,
    a_ref, p_ref, d_ref, pt_ref, select, kn, kp, lhs_h, lhs_l,
    load_sem, ex_send, ex_recv, sum_send, sum_recv, fwd_send, fwd_recv,
):
    s = lax.axis_index("cuts")
    r = lax.axis_index("row")
    odd = lax.rem(s, 2)
    has_lower = s > 0
    has_upper = s < SLICES - 1
    has_slow = jnp.logical_and(has_lower, has_upper)
    paced = jnp.logical_or(s == SLICES // 2 - 1, s == SLICES // 2)
    unpaced = jnp.logical_and(has_slow, jnp.logical_not(paced))
    upper = lax.rem(s + 1, SLICES)
    near = s + 1 - 2 * odd
    far = lax.rem(s + SLICES - 1 + 2 * odd, SLICES)
    near_row = pl.multiple_of(128 - 128 * odd, 64)
    far_row = pl.multiple_of(128 * odd, 64)
    rest_row = pl.multiple_of(64 - 64 * odd, 64)

    load_x = pltpu.make_async_copy(v_hbm, x, load_sem.at[0])
    load_y = pltpu.make_async_copy(i_hbm, y, load_sem.at[1])
    load_x.start()
    load_y.start()

    barrier = pltpu.get_barrier_semaphore()
    for q in (near, far):
        pl.semaphore_signal(barrier, inc=1, device_id=(q, r), device_id_type=MESH)

    def greet(i, carry):
        pl.semaphore_signal(barrier, inc=1, device_id=(s, lax.rem(r + i, PEERS)), device_id_type=MESH)
        return carry

    lax.fori_loop(1, PEERS, greet, 0)

    flags = flags_ref[...].astype(F32)
    row_id = lax.broadcasted_iota(jnp.int32, (SLICES, W), 0)
    before = jnp.sum(jnp.where(row_id < s, flags, 0.0), keepdims=True)
    own_flags = jnp.sum(jnp.where(row_id == s, flags, 0.0), axis=0, keepdims=True)
    earlier = lax.broadcasted_iota(jnp.int32, (W, W), 0) < lax.broadcasted_iota(jnp.int32, (W, W), 1)
    ranks = dot(jnp.broadcast_to(own_flags, (8, W)), jnp.where(earlier, 1.0, 0.0))[0:1]
    slot = ranks + before - (s * KEEP_DEV).astype(F32)
    slot_id = lax.broadcasted_iota(jnp.int32, (W, W), 0).astype(F32)
    select[...] = jnp.where(jnp.logical_and(slot_id == slot, own_flags > 0.5), 1.0, 0.0)
    for ref in (g_hh, g_hl, proj, pack_g, pack_f, pack_s):
        ref[...] = jnp.zeros_like(ref)

    pl.semaphore_wait(barrier, PEERS + 1)

    def lanes(c):
        return pl.ds(pl.multiple_of(c * CHUNK, CHUNK), CHUNK)

    def exchange(kind, c, way):
        return pltpu.make_async_remote_copy(
            src_ref=(v_hbm, i_hbm)[kind].at[pl.ds((near_row, far_row)[way], SHARED), lanes(c)],
            dst_ref=((fv, sv), (fi, si))[kind][way].at[:, lanes(c)],
            send_sem=ex_send.at[kind, way, c],
            recv_sem=ex_recv.at[kind, way, c],
            device_id=((near, far)[way], r),
            device_id_type=MESH,
        )

    def when_slow(action):
        pl.when(has_slow)(action)

    def blend(own, other, row, c):
        mine = own[pl.ds(row, SHARED), lanes(c)]
        own[pl.ds(row, SHARED), lanes(c)] = 0.5 * (mine + other[:, lanes(c)])

    for c in range(CHUNKS):
        when_slow(lambda c=c: exchange(0, c, 1).start())
        exchange(0, c, 0).start()
    for c in range(CHUNKS):
        exchange(1, c, 0).start()
    load_x.wait()

    def gram_step(c, carry):
        exchange(0, c, 0).wait_recv()
        blend(x, fv, near_row, c)

        @pl.when(has_slow)
        def _():
            exchange(0, c, 1).wait_recv()
            blend(x, sv, far_row, c)

        high, low = split(x[:, lanes(c)])
        xh[:, lanes(c)] = high
        xl[:, lanes(c)] = low
        g_hh[...] += dot_rows(high, high)
        g_hl[...] += dot_rows(high, low)

        @pl.when(jnp.logical_and(unpaced, c == CHUNKS - 2))
        def _():
            exchange(1, 0, 1).start()

        return carry

    lax.fori_loop(0, CHUNKS, gram_step, 0)
    for c in range(1, CHUNKS):
        pl.when(unpaced)(lambda c=c: exchange(1, c, 1).start())

    sums = (
        (pack_g, parts_g, mine_g, full_g, PACK[0] // PEERS),
        (pack_f, parts_f, mine_f, full_f, PACK[1] // PEERS),
        (pack_s, parts_s, mine_s, full_s, PACK[2] // PEERS),
    )

    def scatter(which):
        pack, parts, _, _, chunk = sums[which]

        def one(i, carry):
            q = lax.rem(r + i, PEERS)
            pltpu.make_async_remote_copy(
                src_ref=pack.at[pl.ds(pl.multiple_of(q * chunk, 8), chunk), :],
                dst_ref=parts.at[i - 1],
                send_sem=sum_send.at[0, which],
                recv_sem=sum_recv.at[0, which],
                device_id=(s, q),
                device_id_type=MESH,
            ).start()
            return carry

        lax.fori_loop(1, PEERS, one, 0)

    def arrived(phase, which):
        parts = sums[which][1]
        return pltpu.make_async_remote_copy(
            src_ref=parts,
            dst_ref=parts,
            send_sem=sum_send.at[phase, which],
            recv_sem=sum_recv.at[phase, which],
            device_id=(s, lax.rem(r + 1, PEERS)),
            device_id_type=MESH,
        )

    def add_and_gather(which):
        pack, parts, mine, full, chunk = sums[which]
        place = pl.ds(pl.multiple_of(r * chunk, 8), chunk)
        arrived(0, which).wait_recv()
        total = pack[place, :]
        for i in range(PEERS - 1):
            total = total + parts[i]
        mine[...] = total
        full[place, :] = total

        def one(i, carry):
            pltpu.make_async_remote_copy(
                src_ref=mine,
                dst_ref=full.at[place, :],
                send_sem=sum_send.at[1, which],
                recv_sem=sum_recv.at[1, which],
                device_id=(s, lax.rem(r + i, PEERS)),
                device_id_type=MESH,
            ).start()
            return carry

        lax.fori_loop(1, PEERS, one, 0)

    gram = g_hh[...] + (g_hl[...] + g_hl[...].T)
    pack_g[0:W, :] = gram[:, 0:128]
    pack_g[W : W + 64, 0:64] = gram[128:W, 128:W]
    scatter(0)
    for c in range(CHUNKS // 2):
        pl.when(paced)(lambda c=c: exchange(1, c, 1).start())

    load_y.wait()

    def rest_step(c, carry):
        exchange(1, c, 0).wait_recv()
        blend(y, fi, near_row, c)
        high, low = split(y[pl.ds(rest_row, 128), lanes(c)])
        base = xh[:, lanes(c)]
        proj[0:128, :] += dot_rows(high, base) + (dot_rows(high, xl[:, lanes(c)]) + dot_rows(low, base))
        return carry

    lax.fori_loop(0, CHUNKS, rest_step, 0)
    pack_f[0:128, :] = proj[0:128, 0:128]
    pack_f[128:W, 0:64] = proj[0:64, 128:W]
    pack_f[128:W, 64:128] = proj[64:128, 128:W]
    add_and_gather(0)
    scatter(1)
    for c in range(CHUNKS // 2, CHUNKS):
        pl.when(paced)(lambda c=c: exchange(1, c, 1).start())

    def far_step(c, carry):
        @pl.when(has_slow)
        def _():
            exchange(1, c, 1).wait_recv()
            blend(y, si, far_row, c)

        high, low = split(y[pl.ds(far_row, SHARED), lanes(c)])
        base = xh[:, lanes(c)]
        proj[128:W, :] += dot_rows(high, base) + (dot_rows(high, xl[:, lanes(c)]) + dot_rows(low, base))
        return carry

    lax.fori_loop(0, CHUNKS // 2, far_step, 0)
    arrived(1, 0).wait_recv()
    a_ref[:, 0:128] = full_g[0:W, :]
    corner = jnp.concatenate([full_g[128:W, :].T, full_g[W : W + 64, 0:64]], 0)
    a_ref[:, 128:LANES] = jnp.concatenate([corner, jnp.zeros((W, 64), F32)], 1)
    lax.fori_loop(CHUNKS // 2, CHUNKS, far_step, 0)
    pack_s[0:64, :] = proj[128:W, 0:128]
    pack_s[64:128, 0:64] = proj[128:W, 128:W]
    scatter(2)

    def early(c):
        return pltpu.make_async_remote_copy(
            src_ref=x.at[0:128, lanes(c)],
            dst_ref=xp.at[:, lanes(c)],
            send_sem=fwd_send.at[c],
            recv_sem=fwd_recv.at[c],
            device_id=(upper, r),
            device_id_type=MESH,
        )

    @pl.when(has_upper)
    def _():
        early(0).start()

    def sweep_step(step, carry):
        sweep_panel(step, a_ref, p_ref, d_ref)
        return carry

    lax.fori_loop(0, 1, sweep_step, 0)
    add_and_gather(1)
    lax.fori_loop(1, 3, sweep_step, 0)
    add_and_gather(2)

    @pl.when(has_upper)
    def _():
        for c in range(1, EARLY):
            early(c).start()

    lax.fori_loop(3, W // PANEL, sweep_step, 0)

    arrived(1, 1).wait_recv()
    pt_ref[pl.ds(rest_row, 128), 0:128] = full_f[0:128, :]
    pt_ref[pl.ds(rest_row, 64), 128:W] = full_f[128:W, 0:64]
    pt_ref[pl.ds(rest_row + 64, 64), 128:W] = full_f[128:W, 64:128]
    arrived(1, 2).wait_recv()
    pt_ref[pl.ds(far_row, 64), 0:128] = full_s[0:64, :]
    pt_ref[pl.ds(far_row, 64), 128:W] = full_s[64:128, 0:64]
    coeff = dot(pt_ref[...], -a_ref[:, 0:W])
    passed = dot(select[KEEP_DEV:W, :], coeff)
    kn[...] = passed

    late = pltpu.make_async_remote_copy(
        src_ref=kn,
        dst_ref=kp,
        send_sem=fwd_send.at[CHUNKS],
        recv_sem=fwd_recv.at[CHUNKS],
        device_id=(upper, r),
        device_id_type=MESH,
    )

    def product(c):
        place = pl.ds(pl.multiple_of((c - EARLY) * CHUNK, CHUNK), CHUNK)
        return pltpu.make_async_remote_copy(
            src_ref=z_out.at[:, place],
            dst_ref=z_in.at[:, place],
            send_sem=fwd_send.at[c],
            recv_sem=fwd_recv.at[c],
            device_id=(upper, r),
            device_id_type=MESH,
        )

    @pl.when(has_upper)
    def _():
        late.start()
        factor = split(passed)

        def product_step(c, carry):
            z_out[:, pl.ds(pl.multiple_of((c - EARLY) * CHUNK, CHUNK), CHUNK)] = dot_split(
                factor, (xh[:, lanes(c)], xl[:, lanes(c)])
            )
            product(c).start()
            return carry

        lax.fori_loop(EARLY, CHUNKS, product_step, 0)

    high, low = split(coeff)
    lhs_h[0:W, :] = high
    lhs_l[0:W, :] = low
    high, low = split(dot(select[0:KEEP_DEV, :], coeff))
    lhs_h[W : W + KEEP_DEV, :] = high
    lhs_l[W : W + KEEP_DEV, :] = low

    def rotate_step(c, carry):
        both = dot_split((lhs_h[...], lhs_l[...]), (xh[:, lanes(c)], xl[:, lanes(c)]))
        res_ref[:, lanes(c)] = y[:, lanes(c)] - both[0:W]
        kept_ref[:, lanes(c)] = both[W : W + KEEP_DEV]
        return carry

    lax.fori_loop(0, CHUNKS, rotate_step, 0)

    @pl.when(has_lower)
    def _():
        late.wait_recv()
        first = split(kp[:, 0:128])
        last = split(kp[:, 128:W])

        def early_step(c, carry):
            early(c).wait_recv()
            extra = dot_split(first, split(xp[:, lanes(c)]))
            extra = extra + dot_split(last, (xh[0:SHARED, lanes(c)], xl[0:SHARED, lanes(c)]))
            kept_ref[:, lanes(c)] += extra
            return carry

        lax.fori_loop(0, EARLY, early_step, 0)

        def late_step(c, carry):
            product(c).wait_recv()
            kept_ref[:, lanes(c)] += z_in[:, pl.ds(pl.multiple_of((c - EARLY) * CHUNK, CHUNK), CHUNK)]
            return carry

        lax.fori_loop(EARLY, CHUNKS, late_step, 0)

    for kind in range(2):
        for c in range(CHUNKS):
            exchange(kind, c, 0).wait_send()
            when_slow(lambda kind=kind, c=c: exchange(kind, c, 1).wait_send())
    for phase in range(2):
        for which in range(3):
            arrived(phase, which).wait_send()

    @pl.when(has_upper)
    def _():
        late.wait_send()
        for c in range(EARLY):
            early(c).wait_send()
        for c in range(EARLY, CHUNKS):
            product(c).wait_send()


def fused_call(vectors, images, flags):
    shape = jax.ShapeDtypeStruct
    dma = pltpu.SemaphoreType.DMA

    def vmem(*dims, dtype=F32):
        return pltpu.VMEM(dims, dtype)

    big, shared = vmem(W, ROWS), vmem(SHARED, ROWS)
    half = vmem(W, ROWS, dtype=BF16)
    late_rows = vmem(KEEP_DEV, ROWS - EARLY_ROWS)
    chunks = [size // PEERS for size in PACK]
    return pl.pallas_call(
        fused_kernel,
        out_shape=(shape((W, ROWS), F32), shape((KEEP_DEV, ROWS), F32)),
        in_specs=[HBM, HBM, VMEM],
        out_specs=(VMEM, VMEM),
        scratch_shapes=[
            big, big, half, half, shared, shared, shared, shared,
            vmem(2 * SHARED, EARLY_ROWS), late_rows, late_rows,
            vmem(W, W), vmem(W, W), vmem(W, W),
            *[vmem(size, 128) for size in PACK],
            *[vmem(PEERS - 1, chunk, 128) for chunk in chunks],
            *[vmem(chunk, 128) for chunk in chunks],
            *[vmem(size, 128) for size in PACK],
            vmem(W, LANES), vmem(PANEL, LANES), vmem(8, 8, 128), vmem(W, W), vmem(W, W), vmem(KEEP_DEV, W), vmem(KEEP_DEV, W),
            vmem(W + KEEP_DEV, W, dtype=BF16), vmem(W + KEEP_DEV, W, dtype=BF16),
            dma((2,)), dma((2, 2, CHUNKS)), dma((2, 2, CHUNKS)), dma((2, 3)), dma((2, 3)),
            dma((CHUNKS + 1,)), dma((CHUNKS + 1,)),
        ],
        compiler_params=pltpu.CompilerParams(
            collective_id=0, has_side_effects=True, vmem_limit_bytes=VMEM_LIMIT
        ),
        name="fused",
    )(vectors, images, flags)


def on_device(vectors, images, kept_flags):
    residual, kept = fused_call(vectors[0].T, images[0].T, kept_flags)
    return residual.T[None], kept.T[None]


def solution(mesh):
    placed = (P("cuts", "row", None), P("cuts", "row", None), P())
    return jax.shard_map(
        on_device,
        mesh=mesh,
        in_specs=placed,
        out_specs=(P("cuts", "row", None), P("cuts", "row", None)),
        check_vma=False,
    )
```

time: 331 us -> 75.8 us (0.23)
  waiting for transfers between devices: 209 us -> 0 us
  Pallas kernels: 0 us -> 71.4 us
  other arithmetic: 69.4 us -> 0 us
  matrix products: 18.8 us -> 0 us
  between operations: 15.6 us -> 0.65 us
  local copies, waits for them, and re-layouts: 11 us -> 3.52 us
  starting transfers between devices: 5.91 us -> 0 us
    psum x1 -> x0, waiting for transfers between devices: 138 us -> none  [on_device(): gram, projected = lax.psum((gram_local, projected_local), 'row')]
    pallas_call x0 -> x1, Pallas kernels: none -> 71.4 us  [fused_call(): pl.pallas_call(fused_kernel, out_shape=(shape((W, ROWS), F32), shape((KEE...]
    ppermute x3 -> x0, waiting for transfers between devices: 70.8 us -> none  [passed_along(): lax.ppermute(value, axis, [(source, source + steps) for source in range(f...]
    another operation x16 -> x0, other arithmetic: 54.9 us -> none  [the longest x7 31.7 us: solve_coeff(): factor = jnp.linalg.cholesky(gram)]
    dot_general x4 -> x0, matrix products: 13.4 us -> none  [the longest x1 4.69 us: on_device(): jnp.dot(basis, coeff, precision=high, preferred_element_type=jnp.float32)]
    squeeze x2 -> x0, other arithmetic: 6.48 us -> none  [the longest x1 4.57 us: on_device(): new_head = jnp.where(slice_id > 0, 0.5 * (head + from_lower), head)[0]]
    ppermute x3 -> x0, starting transfers between devices: 5.87 us -> none  [passed_along(): lax.ppermute(value, axis, [(source, source + steps) for source in range(f...]
    another operation x8 -> x0, matrix products: 5.39 us -> none  [the longest x3 2.69 us: solve_coeff(): middle = jax.scipy.linalg.solve_triangular(factor, projected, lower=True)]
  transfers between devices with their start and end apart: 4 -> 0, of which waited for: 4 -> 0; matrix products, arithmetic and copies ran while one was open for 2% -> 0% of each run, Pallas kernels for 0% -> 0%
where the time goes in v2:
time: 75.8 us; the launch traced here: 75.6 us
  Pallas kernels  71.4 us (94%)
  local copies, waits for them, and re-layouts  3.52 us (5%)
    pallas_call x1, Pallas kernels, fused_call(): pl.pallas_call(fused_kernel, out_shape=(shape((W, ROWS), F32), shape((KEE...  71.4 us
    unnamed x4, local copies, waits for them, and re-layouts  3.52 us

profile of v2, /device:TPU:4, one launch (start us, length us, event | category | flops | bytes accessed | tf_op | source)
XLA Modules:
  0.0 75.6 jit_solution(10349658876579474509)
XLA Ops:
  0.6 0.0 copy-start
  0.6 0.7 copy-done
  1.3 71.4 %fused.1 = (f32[192,4096]{1,0:T(8,128)S(1)}, f32[96,4096]{1,0:T(8,128)S(1)}) custom-call(f32[192,4096]{1,0:T(8,128)} %bitcast.14, f32[192,4096]{1,0:T(8,128)} %bitcast.15, s32[16,192]{1,0:T(8,128)S(1)} %copy-done), custom_call_target="tpu_custom_call" | custom-call | tf_op jit(solution)/shard_map/fused/pallas_call | solution.py:468
  72.8 1.7 %copy.7 = f32[1,4096,192]{1,2,0:T(8,128)} copy(f32[1,4096,192]{1,2,0:T(8,128)S(1)} %bitcast.12) | data formatting | bytes 6291456
  74.5 1.1 %copy.8 = f32[1,4096,96]{1,2,0:T(8,128)} copy(f32[1,4096,96]{1,2,0:T(8,128)S(1)} %bitcast.13) | data formatting | bytes 3145728
Async XLA Ops:
  0.6 0.7 copy-start

commit v3 on v2

--- a/solution.py
+++ b/solution.py
@@ -13,14 +13,18 @@
 SLICES = 16
 ROWS = 4096
 PEERS = 16
+DEPTH = 8
 CHUNKS = 4
 CHUNK = ROWS // CHUNKS
-EARLY = 2
-EARLY_ROWS = EARLY * CHUNK
+UNITS = 8
+UNIT = ROWS // UNITS
+FIRST = 2
+EARLY = 6
+EARLY_ROWS = EARLY * UNIT
 LANES = 256
 PANEL = 48
 VMEM_LIMIT = 48 << 20
-PACK = (256, 256, 128)
+PACK = (192, 192, 128)
 F32 = jnp.float32
 BF16 = jnp.bfloat16
 HIGH = lax.Precision.HIGHEST
@@ -122,6 +126,7 @@
     res_ref, kept_ref,
     x, y, xh, xl, fv, fi, sv, si, xp, z_out, z_in, g_hh, g_hl, proj,
     pack_g, pack_f, pack_s, parts_g, parts_f, parts_s, mine_g, mine_f, mine_s, full_g, full_f, full_s,
+    other_g, other_f,
     a_ref, p_ref, d_ref, pt_ref, select, kn, kp, lhs_h, lhs_l,
     load_sem, ex_send, ex_recv, sum_send, sum_recv, fwd_send, fwd_recv,
 ):
@@ -131,8 +136,6 @@
     has_lower = s > 0
     has_upper = s < SLICES - 1
     has_slow = jnp.logical_and(has_lower, has_upper)
-    paced = jnp.logical_or(s == SLICES // 2 - 1, s == SLICES // 2)
-    unpaced = jnp.logical_and(has_slow, jnp.logical_not(paced))
     upper = lax.rem(s + 1, SLICES)
     near = s + 1 - 2 * odd
     far = lax.rem(s + SLICES - 1 + 2 * odd, SLICES)
@@ -164,13 +167,16 @@
     slot = ranks + before - (s * KEEP_DEV).astype(F32)
     slot_id = lax.broadcasted_iota(jnp.int32, (W, W), 0).astype(F32)
     select[...] = jnp.where(jnp.logical_and(slot_id == slot, own_flags > 0.5), 1.0, 0.0)
-    for ref in (g_hh, g_hl, proj, pack_g, pack_f, pack_s):
+    for ref in (g_hh, g_hl, proj, pack_s):
         ref[...] = jnp.zeros_like(ref)
 
     pl.semaphore_wait(barrier, PEERS + 1)
 
     def lanes(c):
         return pl.ds(pl.multiple_of(c * CHUNK, CHUNK), CHUNK)
+
+    def unit(c):
+        return pl.ds(pl.multiple_of(c * UNIT, UNIT), UNIT)
 
     def exchange(kind, c, way):
         return pltpu.make_async_remote_copy(
@@ -194,7 +200,9 @@
         exchange(0, c, 0).start()
     for c in range(CHUNKS):
         exchange(1, c, 0).start()
+    when_slow(lambda: exchange(1, 0, 1).start())
     load_x.wait()
+    load_y.wait()
 
     def gram_step(c, carry):
         exchange(0, c, 0).wait_recv()
@@ -211,29 +219,44 @@
         g_hh[...] += dot_rows(high, high)
         g_hl[...] += dot_rows(high, low)
 
-        @pl.when(jnp.logical_and(unpaced, c == CHUNKS - 2))
-        def _():
-            exchange(1, 0, 1).start()
-
+        exchange(1, c, 0).wait_recv()
+        blend(y, fi, near_row, c)
+        rest_high, rest_low = split(y[pl.ds(rest_row, 128), lanes(c)])
+        proj[0:128, :] += dot_rows(rest_high, high) + (dot_rows(rest_high, low) + dot_rows(rest_low, high))
         return carry
 
     lax.fori_loop(0, CHUNKS, gram_step, 0)
-    for c in range(1, CHUNKS):
-        pl.when(unpaced)(lambda c=c: exchange(1, c, 1).start())
-
     sums = (
-        (pack_g, parts_g, mine_g, full_g, PACK[0] // PEERS),
-        (pack_f, parts_f, mine_f, full_f, PACK[1] // PEERS),
-        (pack_s, parts_s, mine_s, full_s, PACK[2] // PEERS),
+        (pack_g, parts_g, mine_g, full_g, other_g, PACK[0] // DEPTH),
+        (pack_f, parts_f, mine_f, full_f, other_f, PACK[1] // DEPTH),
+        (pack_s, parts_s, mine_s, full_s, None, PACK[2] // DEPTH),
     )
+    partner = r + 1 - 2 * lax.rem(r, 2)
+
+    def along_z(i):
+        return lax.rem(r + 2 * i, PEERS)
+
+    def swap(which):
+        pack, _, _, _, other, _ = sums[which]
+        return pltpu.make_async_remote_copy(
+            src_ref=pack,
+            dst_ref=other,
+            send_sem=sum_send.at[2, which],
+            recv_sem=sum_recv.at[2, which],
+            device_id=(s, partner),
+            device_id_type=MESH,
+        )
 
     def scatter(which):
-        pack, parts, _, _, chunk = sums[which]
+        pack, parts, _, _, other, chunk = sums[which]
+        if which < 2:
+            swap(which).wait()
+            pack[...] += other[...]
 
         def one(i, carry):
-            q = lax.rem(r + i, PEERS)
+            q = along_z(i) if which < 2 else lax.rem(r + i, PEERS)
             pltpu.make_async_remote_copy(
-                src_ref=pack.at[pl.ds(pl.multiple_of(q * chunk, 8), chunk), :],
+                src_ref=pack.at[pl.ds(pl.multiple_of((q // 2) * chunk, 8), chunk), :],
                 dst_ref=parts.at[i - 1],
                 send_sem=sum_send.at[0, which],
                 recv_sem=sum_recv.at[0, which],
@@ -242,25 +265,27 @@
             ).start()
             return carry
 
-        lax.fori_loop(1, PEERS, one, 0)
+        lax.fori_loop(1, DEPTH if which < 2 else PEERS, one, 0)
 
     def arrived(phase, which):
         parts = sums[which][1]
+        if phase == 1:
+            parts = parts.at[0 : DEPTH - 1]
         return pltpu.make_async_remote_copy(
             src_ref=parts,
             dst_ref=parts,
             send_sem=sum_send.at[phase, which],
             recv_sem=sum_recv.at[phase, which],
-            device_id=(s, lax.rem(r + 1, PEERS)),
+            device_id=(s, along_z(1)),
             device_id_type=MESH,
         )
 
     def add_and_gather(which):
-        pack, parts, mine, full, chunk = sums[which]
-        place = pl.ds(pl.multiple_of(r * chunk, 8), chunk)
+        pack, parts, mine, full, _, chunk = sums[which]
+        place = pl.ds(pl.multiple_of((r // 2) * chunk, 8), chunk)
         arrived(0, which).wait_recv()
         total = pack[place, :]
-        for i in range(PEERS - 1):
+        for i in range(DEPTH - 1 if which < 2 else PEERS - 1):
             total = total + parts[i]
         mine[...] = total
         full[place, :] = total
@@ -271,38 +296,44 @@
                 dst_ref=full.at[place, :],
                 send_sem=sum_send.at[1, which],
                 recv_sem=sum_recv.at[1, which],
-                device_id=(s, lax.rem(r + i, PEERS)),
+                device_id=(s, along_z(i)),
                 device_id_type=MESH,
             ).start()
             return carry
 
-        lax.fori_loop(1, PEERS, one, 0)
+        lax.fori_loop(1, DEPTH, one, 0)
 
     gram = g_hh[...] + (g_hl[...] + g_hl[...].T)
-    pack_g[0:W, :] = gram[:, 0:128]
-    pack_g[W : W + 64, 0:64] = gram[128:W, 128:W]
-    scatter(0)
-    for c in range(CHUNKS // 2):
-        pl.when(paced)(lambda c=c: exchange(1, c, 1).start())
-
-    load_y.wait()
-
-    def rest_step(c, carry):
-        exchange(1, c, 0).wait_recv()
-        blend(y, fi, near_row, c)
-        high, low = split(y[pl.ds(rest_row, 128), lanes(c)])
-        base = xh[:, lanes(c)]
-        proj[0:128, :] += dot_rows(high, base) + (dot_rows(high, xl[:, lanes(c)]) + dot_rows(low, base))
-        return carry
-
-    lax.fori_loop(0, CHUNKS, rest_step, 0)
+    pack_g[:, 0:64] = gram[:, 0:64]
+    pack_g[64:W, 64:128] = gram[64:W, 64:128]
+    pack_g[0:64, 64:128] = gram[128:W, 128:W]
+    swap(0).start()
     pack_f[0:128, :] = proj[0:128, 0:128]
     pack_f[128:W, 0:64] = proj[0:64, 128:W]
     pack_f[128:W, 64:128] = proj[64:128, 128:W]
+    swap(1).start()
+    for c in range(1, CHUNKS):
+        when_slow(lambda c=c: exchange(1, c, 1).start())
+
+    def early(c):
+        return pltpu.make_async_remote_copy(
+            src_ref=x.at[0:128, unit(c)],
+            dst_ref=xp.at[:, unit(c)],
+            send_sem=fwd_send.at[c],
+            recv_sem=fwd_recv.at[c],
+            device_id=(upper, r),
+            device_id_type=MESH,
+        )
+
+    @pl.when(has_upper)
+    def _():
+        for c in range(FIRST):
+            early(c).start()
+
+    scatter(0)
+    scatter(1)
     add_and_gather(0)
-    scatter(1)
-    for c in range(CHUNKS // 2, CHUNKS):
-        pl.when(paced)(lambda c=c: exchange(1, c, 1).start())
+    add_and_gather(1)
 
     def far_step(c, carry):
         @pl.when(has_slow)
@@ -317,43 +348,27 @@
 
     lax.fori_loop(0, CHUNKS // 2, far_step, 0)
     arrived(1, 0).wait_recv()
-    a_ref[:, 0:128] = full_g[0:W, :]
-    corner = jnp.concatenate([full_g[128:W, :].T, full_g[W : W + 64, 0:64]], 0)
+    a_ref[64:W, 0:128] = full_g[64:W, :]
+    a_ref[0:64, 0:128] = jnp.concatenate([full_g[0:64, 0:64], full_g[64:128, 0:64].T], 1)
+    corner = jnp.concatenate([full_g[128:W, :].T, full_g[0:64, 64:128]], 0)
     a_ref[:, 128:LANES] = jnp.concatenate([corner, jnp.zeros((W, 64), F32)], 1)
     lax.fori_loop(CHUNKS // 2, CHUNKS, far_step, 0)
     pack_s[0:64, :] = proj[128:W, 0:128]
     pack_s[64:128, 0:64] = proj[128:W, 128:W]
     scatter(2)
 
-    def early(c):
-        return pltpu.make_async_remote_copy(
-            src_ref=x.at[0:128, lanes(c)],
-            dst_ref=xp.at[:, lanes(c)],
-            send_sem=fwd_send.at[c],
-            recv_sem=fwd_recv.at[c],
-            device_id=(upper, r),
-            device_id_type=MESH,
-        )
-
     @pl.when(has_upper)
     def _():
-        early(0).start()
+        for c in range(FIRST, EARLY):
+            early(c).start()
 
     def sweep_step(step, carry):
         sweep_panel(step, a_ref, p_ref, d_ref)
         return carry
 
-    lax.fori_loop(0, 1, sweep_step, 0)
-    add_and_gather(1)
-    lax.fori_loop(1, 3, sweep_step, 0)
+    lax.fori_loop(0, 2, sweep_step, 0)
     add_and_gather(2)
-
-    @pl.when(has_upper)
-    def _():
-        for c in range(1, EARLY):
-            early(c).start()
-
-    lax.fori_loop(3, W // PANEL, sweep_step, 0)
+    lax.fori_loop(2, W // PANEL, sweep_step, 0)
 
     arrived(1, 1).wait_recv()
     pt_ref[pl.ds(rest_row, 128), 0:128] = full_f[0:128, :]
@@ -369,14 +384,14 @@
     late = pltpu.make_async_remote_copy(
         src_ref=kn,
         dst_ref=kp,
-        send_sem=fwd_send.at[CHUNKS],
-        recv_sem=fwd_recv.at[CHUNKS],
+        send_sem=fwd_send.at[UNITS],
+        recv_sem=fwd_recv.at[UNITS],
         device_id=(upper, r),
         device_id_type=MESH,
     )
 
     def product(c):
-        place = pl.ds(pl.multiple_of((c - EARLY) * CHUNK, CHUNK), CHUNK)
+        place = unit(c - EARLY)
         return pltpu.make_async_remote_copy(
             src_ref=z_out.at[:, place],
             dst_ref=z_in.at[:, place],
@@ -392,13 +407,11 @@
         factor = split(passed)
 
         def product_step(c, carry):
-            z_out[:, pl.ds(pl.multiple_of((c - EARLY) * CHUNK, CHUNK), CHUNK)] = dot_split(
-                factor, (xh[:, lanes(c)], xl[:, lanes(c)])
-            )
+            z_out[:, unit(c - EARLY)] = dot_split(factor, (xh[:, unit(c)], xl[:, unit(c)]))
             product(c).start()
             return carry
 
-        lax.fori_loop(EARLY, CHUNKS, product_step, 0)
+        lax.fori_loop(EARLY, UNITS, product_step, 0)
 
     high, low = split(coeff)
     lhs_h[0:W, :] = high
@@ -423,19 +436,19 @@
 
         def early_step(c, carry):
             early(c).wait_recv()
-            extra = dot_split(first, split(xp[:, lanes(c)]))
-            extra = extra + dot_split(last, (xh[0:SHARED, lanes(c)], xl[0:SHARED, lanes(c)]))
-            kept_ref[:, lanes(c)] += extra
+            extra = dot_split(first, split(xp[:, unit(c)]))
+            extra = extra + dot_split(last, (xh[0:SHARED, unit(c)], xl[0:SHARED, unit(c)]))
+            kept_ref[:, unit(c)] += extra
             return carry
 
         lax.fori_loop(0, EARLY, early_step, 0)
 
         def late_step(c, carry):
             product(c).wait_recv()
-            kept_ref[:, lanes(c)] += z_in[:, pl.ds(pl.multiple_of((c - EARLY) * CHUNK, CHUNK), CHUNK)]
+            kept_ref[:, unit(c)] += z_in[:, unit(c - EARLY)]
             return carry
 
-        lax.fori_loop(EARLY, CHUNKS, late_step, 0)
+        lax.fori_loop(EARLY, UNITS, late_step, 0)
 
     for kind in range(2):
         for c in range(CHUNKS):
@@ -450,7 +463,7 @@
         late.wait_send()
         for c in range(EARLY):
             early(c).wait_send()
-        for c in range(EARLY, CHUNKS):
+        for c in range(EARLY, UNITS):
             product(c).wait_send()
 
 
@@ -464,7 +477,7 @@
     big, shared = vmem(W, ROWS), vmem(SHARED, ROWS)
     half = vmem(W, ROWS, dtype=BF16)
     late_rows = vmem(KEEP_DEV, ROWS - EARLY_ROWS)
-    chunks = [size // PEERS for size in PACK]
+    chunks = [size // DEPTH for size in PACK]
     return pl.pallas_call(
         fused_kernel,
         out_shape=(shape((W, ROWS), F32), shape((KEEP_DEV, ROWS), F32)),
@@ -475,13 +488,14 @@
             vmem(2 * SHARED, EARLY_ROWS), late_rows, late_rows,
             vmem(W, W), vmem(W, W), vmem(W, W),
             *[vmem(size, 128) for size in PACK],
-            *[vmem(PEERS - 1, chunk, 128) for chunk in chunks],
+            *[vmem(count - 1, chunk, 128) for count, chunk in zip((DEPTH, DEPTH, PEERS), chunks)],
             *[vmem(chunk, 128) for chunk in chunks],
             *[vmem(size, 128) for size in PACK],
+            *[vmem(size, 128) for size in PACK[0:2]],
             vmem(W, LANES), vmem(PANEL, LANES), vmem(8, 8, 128), vmem(W, W), vmem(W, W), vmem(KEEP_DEV, W), vmem(KEEP_DEV, W),
             vmem(W + KEEP_DEV, W, dtype=BF16), vmem(W + KEEP_DEV, W, dtype=BF16),
-            dma((2,)), dma((2, 2, CHUNKS)), dma((2, 2, CHUNKS)), dma((2, 3)), dma((2, 3)),
-            dma((CHUNKS + 1,)), dma((CHUNKS + 1,)),
+            dma((2,)), dma((2, 2, CHUNKS)), dma((2, 2, CHUNKS)), dma((3, 3)), dma((3, 3)),
+            dma((UNITS + 1,)), dma((UNITS + 1,)),
         ],
         compiler_params=pltpu.CompilerParams(
             collective_id=0, has_side_effects=True, vmem_limit_bytes=VMEM_LIMIT

time: 75.8 us -> 67.9 us (0.90)
  Pallas kernels: 71.4 us -> 63.6 us
    pallas_call x1, Pallas kernels: 71.4 us -> 63.6 us  [fused_call(): pl.pallas_call(fused_kernel, out_shape=(shape((W, ROWS), F32), shape((KEE...]
where the time goes in v3:
time: 67.9 us; the launch traced here: 67.7 us
  Pallas kernels  63.6 us (94%)
  local copies, waits for them, and re-layouts  3.52 us (5%)
    pallas_call x1, Pallas kernels, fused_call(): pl.pallas_call(fused_kernel, out_shape=(shape((W, ROWS), F32), shape((KEE...  63.6 us
    unnamed x4, local copies, waits for them, and re-layouts  3.52 us

profile of v3, /device:TPU:4, one launch (start us, length us, event | category | flops | bytes accessed | tf_op | source)
XLA Modules:
  0.0 67.7 jit_solution(9393827912931775636)
XLA Ops:
  0.6 0.0 copy-start
  0.6 0.7 %copy-done = s32[16,192]{1,0:T(8,128)S(1)} copy-done((s32[16,192]{1,0:T(8,128)S(1)}, s32[16,192]{1,0:T(8,128)}, u32[]{:S(2)}) %copy-start) | copy-done | bytes 12312
  1.3 63.6 %fused.1 = (f32[192,4096]{1,0:T(8,128)S(1)}, f32[96,4096]{1,0:T(8,128)S(1)}) custom-call(f32[192,4096]{1,0:T(8,128)} %bitcast.14, f32[192,4096]{1,0:T(8,128)} %bitcast.15, s32[16,192]{1,0:T(8,128)S(1)} %copy-done), custom_call_target="tpu_custom_call" | custom-call | tf_op jit(solution)/shard_map/fused/pallas_call | solution.py:481
  64.9 1.7 %copy.7 = f32[1,4096,192]{1,2,0:T(8,128)} copy(f32[1,4096,192]{1,2,0:T(8,128)S(1)} %bitcast.12) | data formatting | bytes 6291456
  66.6 1.1 %copy.8 = f32[1,4096,96]{1,2,0:T(8,128)} copy(f32[1,4096,96]{1,2,0:T(8,128)S(1)} %bitcast.13) | data formatting | bytes 3145728
Async XLA Ops:
  0.6 0.7 %copy-start = (s32[16,192]{1,0:T(8,128)S(1)}, s32[16,192]{1,0:T(8,128)}, u32[]{:S(2)}) copy-start(s32[16,192]{1,0:T(8,128)} %flags_ref.1) | copy-start | bytes 36868

commit v4 on v3

--- a/solution.py
+++ b/solution.py
@@ -18,8 +18,11 @@
 CHUNK = ROWS // CHUNKS
 UNITS = 8
 UNIT = ROWS // UNITS
-FIRST = 2
-EARLY = 6
+FIRST = 3
+EARLY = 7
+RELAYED = 4
+SOURCE = SLICES // 2 - 1
+TARGET = SLICES // 2
 EARLY_ROWS = EARLY * UNIT
 LANES = 256
 PANEL = 48
@@ -128,7 +131,7 @@
     pack_g, pack_f, pack_s, parts_g, parts_f, parts_s, mine_g, mine_f, mine_s, full_g, full_f, full_s,
     other_g, other_f,
     a_ref, p_ref, d_ref, pt_ref, select, kn, kp, lhs_h, lhs_l,
-    load_sem, ex_send, ex_recv, sum_send, sum_recv, fwd_send, fwd_recv,
+    load_sem, ex_send, ex_recv, sum_send, sum_recv, fwd_send, fwd_recv, relay_send,
 ):
     s = lax.axis_index("cuts")
     r = lax.axis_index("row")
@@ -158,6 +161,51 @@
 
     lax.fori_loop(1, PEERS, greet, 0)
 
+    is_source = s == SOURCE
+    at_ends = jnp.logical_or(is_source, s == TARGET)
+
+    @pl.when(s == 0)
+    def _():
+        for q in (SOURCE, TARGET):
+            pl.semaphore_signal(barrier, inc=1, device_id=(q, r), device_id_type=MESH)
+
+    @pl.when(at_ends)
+    def _():
+        pl.semaphore_signal(barrier, inc=1, device_id=(0, r), device_id_type=MESH)
+
+
+    pl.semaphore_wait(barrier, PEERS + 1 + jnp.where(s == 0, 2, jnp.where(at_ends, 1, 0)))
+
+    def lanes(c):
+        return pl.ds(pl.multiple_of(c * CHUNK, CHUNK), CHUNK)
+
+    def unit(c):
+        return pl.ds(pl.multiple_of(c * UNIT, UNIT), UNIT)
+
+    def exchange(kind, c, way):
+        return pltpu.make_async_remote_copy(
+            src_ref=(v_hbm, i_hbm)[kind].at[pl.ds((near_row, far_row)[way], SHARED), lanes(c)],
+            dst_ref=((fv, sv), (fi, si))[kind][way].at[:, lanes(c)],
+            send_sem=ex_send.at[kind, way, c],
+            recv_sem=ex_recv.at[kind, way, c],
+            device_id=((near, far)[way], r),
+            device_id_type=MESH,
+        )
+
+    def when_slow(action):
+        pl.when(has_slow)(action)
+
+    def blend(own, other, row, c):
+        mine = own[pl.ds(row, SHARED), lanes(c)]
+        own[pl.ds(row, SHARED), lanes(c)] = 0.5 * (mine + other[:, lanes(c)])
+
+    for c in range(CHUNKS):
+        when_slow(lambda c=c: exchange(0, c, 1).start())
+        exchange(0, c, 0).start()
+    for c in range(CHUNKS):
+        exchange(1, c, 0).start()
+    when_slow(lambda: exchange(1, 0, 1).start())
+
     flags = flags_ref[...].astype(F32)
     row_id = lax.broadcasted_iota(jnp.int32, (SLICES, W), 0)
     before = jnp.sum(jnp.where(row_id < s, flags, 0.0), keepdims=True)
@@ -170,37 +218,6 @@
     for ref in (g_hh, g_hl, proj, pack_s):
         ref[...] = jnp.zeros_like(ref)
 
-    pl.semaphore_wait(barrier, PEERS + 1)
-
-    def lanes(c):
-        return pl.ds(pl.multiple_of(c * CHUNK, CHUNK), CHUNK)
-
-    def unit(c):
-        return pl.ds(pl.multiple_of(c * UNIT, UNIT), UNIT)
-
-    def exchange(kind, c, way):
-        return pltpu.make_async_remote_copy(
-            src_ref=(v_hbm, i_hbm)[kind].at[pl.ds((near_row, far_row)[way], SHARED), lanes(c)],
-            dst_ref=((fv, sv), (fi, si))[kind][way].at[:, lanes(c)],
-            send_sem=ex_send.at[kind, way, c],
-            recv_sem=ex_recv.at[kind, way, c],
-            device_id=((near, far)[way], r),
-            device_id_type=MESH,
-        )
-
-    def when_slow(action):
-        pl.when(has_slow)(action)
-
-    def blend(own, other, row, c):
-        mine = own[pl.ds(row, SHARED), lanes(c)]
-        own[pl.ds(row, SHARED), lanes(c)] = 0.5 * (mine + other[:, lanes(c)])
-
-    for c in range(CHUNKS):
-        when_slow(lambda c=c: exchange(0, c, 1).start())
-        exchange(0, c, 0).start()
-    for c in range(CHUNKS):
-        exchange(1, c, 0).start()
-    when_slow(lambda: exchange(1, 0, 1).start())
     load_x.wait()
     load_y.wait()
 
@@ -237,9 +254,9 @@
         return lax.rem(r + 2 * i, PEERS)
 
     def swap(which):
-        pack, _, _, _, other, _ = sums[which]
+        pack, _, mine, _, other, _ = sums[which]
         return pltpu.make_async_remote_copy(
-            src_ref=pack,
+            src_ref=(pack, mine)[which],
             dst_ref=other,
             send_sem=sum_send.at[2, which],
             recv_sem=sum_recv.at[2, which],
@@ -249,8 +266,8 @@
 
     def scatter(which):
         pack, parts, _, _, other, chunk = sums[which]
-        if which < 2:
-            swap(which).wait()
+        if which == 0:
+            swap(0).wait()
             pack[...] += other[...]
 
         def one(i, carry):
@@ -280,15 +297,18 @@
             device_id_type=MESH,
         )
 
-    def add_and_gather(which):
-        pack, parts, mine, full, _, chunk = sums[which]
-        place = pl.ds(pl.multiple_of((r // 2) * chunk, 8), chunk)
+    def add_up(which):
+        pack, parts, mine, _, _, chunk = sums[which]
         arrived(0, which).wait_recv()
-        total = pack[place, :]
+        total = pack[pl.ds(pl.multiple_of((r // 2) * chunk, 8), chunk), :]
         for i in range(DEPTH - 1 if which < 2 else PEERS - 1):
             total = total + parts[i]
         mine[...] = total
-        full[place, :] = total
+
+    def gather(which):
+        _, _, mine, full, _, chunk = sums[which]
+        place = pl.ds(pl.multiple_of((r // 2) * chunk, 8), chunk)
+        full[place, :] = mine[...]
 
         def one(i, carry):
             pltpu.make_async_remote_copy(
@@ -311,29 +331,47 @@
     pack_f[0:128, :] = proj[0:128, 0:128]
     pack_f[128:W, 0:64] = proj[0:64, 128:W]
     pack_f[128:W, 64:128] = proj[64:128, 128:W]
-    swap(1).start()
+    scatter(1)
     for c in range(1, CHUNKS):
         when_slow(lambda c=c: exchange(1, c, 1).start())
 
-    def early(c):
+    def early(c, to):
         return pltpu.make_async_remote_copy(
             src_ref=x.at[0:128, unit(c)],
             dst_ref=xp.at[:, unit(c)],
             send_sem=fwd_send.at[c],
             recv_sem=fwd_recv.at[c],
-            device_id=(upper, r),
+            device_id=(to, r),
             device_id_type=MESH,
         )
 
-    @pl.when(has_upper)
+    def relay(c):
+        return pltpu.make_async_remote_copy(
+            src_ref=xp.at[:, unit(c)],
+            dst_ref=xp.at[:, unit(c)],
+            send_sem=relay_send.at[c],
+            recv_sem=fwd_recv.at[c],
+            device_id=(TARGET, r),
+            device_id_type=MESH,
+        )
+
+    sends_on = jnp.logical_and(has_upper, jnp.logical_not(is_source))
+
+    @pl.when(is_source)
+    def _():
+        for c in range(RELAYED):
+            early(c, 0).start()
+
+    @pl.when(sends_on)
     def _():
         for c in range(FIRST):
-            early(c).start()
+            early(c, upper).start()
 
     scatter(0)
-    scatter(1)
-    add_and_gather(0)
-    add_and_gather(1)
+    add_up(1)
+    swap(1).start()
+    add_up(0)
+    gather(0)
 
     def far_step(c, carry):
         @pl.when(has_slow)
@@ -357,17 +395,32 @@
     pack_s[64:128, 0:64] = proj[128:W, 128:W]
     scatter(2)
 
-    @pl.when(has_upper)
+    @pl.when(is_source)
+    def _():
+        for c in range(RELAYED, EARLY):
+            early(c, upper).start()
+
+    @pl.when(sends_on)
     def _():
         for c in range(FIRST, EARLY):
-            early(c).start()
+            early(c, upper).start()
+
+    @pl.when(s == 0)
+    def _():
+        for c in range(RELAYED):
+            early(c, upper).wait_recv()
+            relay(c).start()
 
     def sweep_step(step, carry):
         sweep_panel(step, a_ref, p_ref, d_ref)
         return carry
 
     lax.fori_loop(0, 2, sweep_step, 0)
-    add_and_gather(2)
+    swap(1).wait()
+    mine_f[...] += other_f[...]
+    gather(1)
+    add_up(2)
+    gather(2)
     lax.fori_loop(2, W // PANEL, sweep_step, 0)
 
     arrived(1, 1).wait_recv()
@@ -435,7 +488,7 @@
         last = split(kp[:, 128:W])
 
         def early_step(c, carry):
-            early(c).wait_recv()
+            early(c, upper).wait_recv()
             extra = dot_split(first, split(xp[:, unit(c)]))
             extra = extra + dot_split(last, (xh[0:SHARED, unit(c)], xl[0:SHARED, unit(c)]))
             kept_ref[:, unit(c)] += extra
@@ -458,11 +511,16 @@
         for which in range(3):
             arrived(phase, which).wait_send()
 
+    @pl.when(s == 0)
+    def _():
+        for c in range(RELAYED):
+            relay(c).wait_send()
+
     @pl.when(has_upper)
     def _():
         late.wait_send()
         for c in range(EARLY):
-            early(c).wait_send()
+            early(c, upper).wait_send()
         for c in range(EARLY, UNITS):
             product(c).wait_send()
 
@@ -491,11 +549,11 @@
             *[vmem(count - 1, chunk, 128) for count, chunk in zip((DEPTH, DEPTH, PEERS), chunks)],
             *[vmem(chunk, 128) for chunk in chunks],
             *[vmem(size, 128) for size in PACK],
-            *[vmem(size, 128) for size in PACK[0:2]],
+            vmem(PACK[0], 128), vmem(chunks[1], 128),
             vmem(W, LANES), vmem(PANEL, LANES), vmem(8, 8, 128), vmem(W, W), vmem(W, W), vmem(KEEP_DEV, W), vmem(KEEP_DEV, W),
             vmem(W + KEEP_DEV, W, dtype=BF16), vmem(W + KEEP_DEV, W, dtype=BF16),
             dma((2,)), dma((2, 2, CHUNKS)), dma((2, 2, CHUNKS)), dma((3, 3)), dma((3, 3)),
-            dma((UNITS + 1,)), dma((UNITS + 1,)),
+            dma((UNITS + 1,)), dma((UNITS + 1,)), dma((RELAYED,)),
         ],
         compiler_params=pltpu.CompilerParams(
             collective_id=0, has_side_effects=True, vmem_limit_bytes=VMEM_LIMIT

time: 67.9 us -> 62.4 us (0.919); the launches traced: 67.7 us -> 61.5 us
  Pallas kernels: 63.6 us -> 57.4 us
    pallas_call x1, Pallas kernels: 63.6 us -> 57.4 us  [fused_call(): pl.pallas_call(fused_kernel, out_shape=(shape((W, ROWS), F32), shape((KEE...]
where the time goes in v4:
time: 62.4 us; the launch traced here: 61.5 us
  Pallas kernels  57.4 us (92%)
  local copies, waits for them, and re-layouts  3.52 us (6%)
  between operations  0.65 us (1%)
    pallas_call x1, Pallas kernels, fused_call(): pl.pallas_call(fused_kernel, out_shape=(shape((W, ROWS), F32), shape((KEE...  57.4 us
    unnamed x4, local copies, waits for them, and re-layouts  3.52 us

profile of v4, /device:TPU:4, one launch (start us, length us, event | category | flops | bytes accessed | tf_op | source)
XLA Modules:
  0.0 61.5 jit_solution(6765758356271154489)
XLA Ops:
  0.6 0.0 copy-start
  0.6 0.7 %copy-done = s32[16,192]{1,0:T(8,128)S(1)} copy-done((s32[16,192]{1,0:T(8,128)S(1)}, s32[16,192]{1,0:T(8,128)}, u32[]{:S(2)}) %copy-start) | copy-done | bytes 12312
  1.3 57.4 %fused.1 = (f32[192,4096]{1,0:T(8,128)S(1)}, f32[96,4096]{1,0:T(8,128)S(1)}) custom-call(f32[192,4096]{1,0:T(8,128)} %bitcast.14, f32[192,4096]{1,0:T(8,128)} %bitcast.15, s32[16,192]{1,0:T(8,128)S(1)} %copy-done), custom_call_target="tpu_custom_call" | custom-call | tf_op jit(solution)/shard_map/fused/pallas_call | solution.py:539
  58.7 1.7 %copy.7 = f32[1,4096,192]{1,2,0:T(8,128)} copy(f32[1,4096,192]{1,2,0:T(8,128)S(1)} %bitcast.12) | data formatting | bytes 6291456
  60.4 1.1 %copy.8 = f32[1,4096,96]{1,2,0:T(8,128)} copy(f32[1,4096,96]{1,2,0:T(8,128)S(1)} %bitcast.13) | data formatting | bytes 3145728
Async XLA Ops:
  0.6 0.7 %copy-start = (s32[16,192]{1,0:T(8,128)S(1)}, s32[16,192]{1,0:T(8,128)}, u32[]{:S(2)}) copy-start(s32[16,192]{1,0:T(8,128)} %flags_ref.1) | copy-start | bytes 36868

commit v5 on v4

--- a/solution.py
+++ b/solution.py
@@ -19,11 +19,11 @@
 UNITS = 8
 UNIT = ROWS // UNITS
 FIRST = 3
-EARLY = 7
+EARLY = 6
 RELAYED = 4
 SOURCE = SLICES // 2 - 1
 TARGET = SLICES // 2
-EARLY_ROWS = EARLY * UNIT
+EARLY_ROWS = (EARLY + 1) * UNIT
 LANES = 256
 PANEL = 48
 VMEM_LIMIT = 48 << 20
@@ -125,13 +125,13 @@
 
 
 def fused_kernel(
-    v_hbm, i_hbm, flags_ref,
+    v_hbm, i_hbm, flags_hbm,
     res_ref, kept_ref,
     x, y, xh, xl, fv, fi, sv, si, xp, z_out, z_in, g_hh, g_hl, proj,
     pack_g, pack_f, pack_s, parts_g, parts_f, parts_s, mine_g, mine_f, mine_s, full_g, full_f, full_s,
     other_g, other_f,
     a_ref, p_ref, d_ref, pt_ref, select, kn, kp, lhs_h, lhs_l,
-    load_sem, ex_send, ex_recv, sum_send, sum_recv, fwd_send, fwd_recv, relay_send,
+    flags_ref, load_sem, ex_send, ex_recv, sum_send, sum_recv, fwd_send, fwd_recv, relay_send,
 ):
     s = lax.axis_index("cuts")
     r = lax.axis_index("row")
@@ -148,6 +148,8 @@
 
     load_x = pltpu.make_async_copy(v_hbm, x, load_sem.at[0])
     load_y = pltpu.make_async_copy(i_hbm, y, load_sem.at[1])
+    load_flags = pltpu.make_async_copy(flags_hbm, flags_ref, load_sem.at[2])
+    load_flags.start()
     load_x.start()
     load_y.start()
 
@@ -206,6 +208,7 @@
         exchange(1, c, 0).start()
     when_slow(lambda: exchange(1, 0, 1).start())
 
+    load_flags.wait()
     flags = flags_ref[...].astype(F32)
     row_id = lax.broadcasted_iota(jnp.int32, (SLICES, W), 0)
     before = jnp.sum(jnp.where(row_id < s, flags, 0.0), keepdims=True)
@@ -356,6 +359,8 @@
         )
 
     sends_on = jnp.logical_and(has_upper, jnp.logical_not(is_source))
+    sent_early = EARLY + jnp.where(is_source, 1, 0)
+    got_early = EARLY + jnp.where(s == TARGET, 1, 0)
 
     @pl.when(is_source)
     def _():
@@ -384,32 +389,32 @@
         proj[128:W, :] += dot_rows(high, base) + (dot_rows(high, xl[:, lanes(c)]) + dot_rows(low, base))
         return carry
 
-    lax.fori_loop(0, CHUNKS // 2, far_step, 0)
+    lax.fori_loop(0, CHUNKS, far_step, 0)
+    pack_s[0:64, :] = proj[128:W, 0:128]
+    pack_s[64:128, 0:64] = proj[128:W, 128:W]
+    scatter(2)
+
+    @pl.when(is_source)
+    def _():
+        for c in range(RELAYED, EARLY + 1):
+            early(c, upper).start()
+
+    @pl.when(sends_on)
+    def _():
+        for c in range(FIRST, EARLY):
+            early(c, upper).start()
+
+    @pl.when(s == 0)
+    def _():
+        for c in range(RELAYED):
+            early(c, upper).wait_recv()
+            relay(c).start()
+
     arrived(1, 0).wait_recv()
     a_ref[64:W, 0:128] = full_g[64:W, :]
     a_ref[0:64, 0:128] = jnp.concatenate([full_g[0:64, 0:64], full_g[64:128, 0:64].T], 1)
     corner = jnp.concatenate([full_g[128:W, :].T, full_g[0:64, 64:128]], 0)
     a_ref[:, 128:LANES] = jnp.concatenate([corner, jnp.zeros((W, 64), F32)], 1)
-    lax.fori_loop(CHUNKS // 2, CHUNKS, far_step, 0)
-    pack_s[0:64, :] = proj[128:W, 0:128]
-    pack_s[64:128, 0:64] = proj[128:W, 128:W]
-    scatter(2)
-
-    @pl.when(is_source)
-    def _():
-        for c in range(RELAYED, EARLY):
-            early(c, upper).start()
-
-    @pl.when(sends_on)
-    def _():
-        for c in range(FIRST, EARLY):
-            early(c, upper).start()
-
-    @pl.when(s == 0)
-    def _():
-        for c in range(RELAYED):
-            early(c, upper).wait_recv()
-            relay(c).start()
 
     def sweep_step(step, carry):
         sweep_panel(step, a_ref, p_ref, d_ref)
@@ -464,7 +469,7 @@
             product(c).start()
             return carry
 
-        lax.fori_loop(EARLY, UNITS, product_step, 0)
+        lax.fori_loop(sent_early, UNITS, product_step, 0)
 
     high, low = split(coeff)
     lhs_h[0:W, :] = high
@@ -494,14 +499,14 @@
             kept_ref[:, unit(c)] += extra
             return carry
 
-        lax.fori_loop(0, EARLY, early_step, 0)
+        lax.fori_loop(0, got_early, early_step, 0)
 
         def late_step(c, carry):
             product(c).wait_recv()
             kept_ref[:, unit(c)] += z_in[:, unit(c - EARLY)]
             return carry
 
-        lax.fori_loop(EARLY, UNITS, late_step, 0)
+        lax.fori_loop(got_early, UNITS, late_step, 0)
 
     for kind in range(2):
         for c in range(CHUNKS):
@@ -521,8 +526,16 @@
         late.wait_send()
         for c in range(EARLY):
             early(c, upper).wait_send()
-        for c in range(EARLY, UNITS):
+        for c in range(EARLY + 1, UNITS):
             product(c).wait_send()
+
+    @pl.when(is_source)
+    def _():
+        early(EARLY, upper).wait_send()
+
+    @pl.when(sends_on)
+    def _():
+        product(EARLY).wait_send()
 
 
 def fused_call(vectors, images, flags):
@@ -534,12 +547,12 @@
 
     big, shared = vmem(W, ROWS), vmem(SHARED, ROWS)
     half = vmem(W, ROWS, dtype=BF16)
-    late_rows = vmem(KEEP_DEV, ROWS - EARLY_ROWS)
+    late_rows = vmem(KEEP_DEV, (UNITS - EARLY) * UNIT)
     chunks = [size // DEPTH for size in PACK]
     return pl.pallas_call(
         fused_kernel,
         out_shape=(shape((W, ROWS), F32), shape((KEEP_DEV, ROWS), F32)),
-        in_specs=[HBM, HBM, VMEM],
+        in_specs=[HBM, HBM, HBM],
         out_specs=(VMEM, VMEM),
         scratch_shapes=[
             big, big, half, half, shared, shared, shared, shared,
@@ -552,7 +565,7 @@
             vmem(PACK[0], 128), vmem(chunks[1], 128),
             vmem(W, LANES), vmem(PANEL, LANES), vmem(8, 8, 128), vmem(W, W), vmem(W, W), vmem(KEEP_DEV, W), vmem(KEEP_DEV, W),
             vmem(W + KEEP_DEV, W, dtype=BF16), vmem(W + KEEP_DEV, W, dtype=BF16),
-            dma((2,)), dma((2, 2, CHUNKS)), dma((2, 2, CHUNKS)), dma((3, 3)), dma((3, 3)),
+            vmem(SLICES, W, dtype=jnp.int32), dma((3,)), dma((2, 2, CHUNKS)), dma((2, 2, CHUNKS)), dma((3, 3)), dma((3, 3)),
             dma((UNITS + 1,)), dma((UNITS + 1,)), dma((RELAYED,)),
         ],
         compiler_params=pltpu.CompilerParams(
@@ -563,6 +576,7 @@
 
 
 def on_device(vectors, images, kept_flags):
+    kept_flags = pltpu.with_memory_space_constraint(kept_flags, pltpu.HBM)
     residual, kept = fused_call(vectors[0].T, images[0].T, kept_flags)
     return residual.T[None], kept.T[None]
 

time: 62.4 us -> 61.2 us (0.981)
  local copies, waits for them, and re-layouts: 3.52 us -> 2.81 us
    unnamed x4 -> x2, local copies, waits for them, and re-layouts: 3.52 us -> 2.81 us
where the time goes in v5:
time: 61.2 us; the launch traced here: 60.5 us
  Pallas kernels  57.1 us (93%)
  local copies, waits for them, and re-layouts  2.81 us (5%)
  between operations  0.64 us (1%)
    pallas_call x1, Pallas kernels, fused_call(): pl.pallas_call(fused_kernel, out_shape=(shape((W, ROWS), F32), shape((KEE...  57.1 us
    unnamed x2, local copies, waits for them, and re-layouts  2.81 us

profile of v5, /device:TPU:4, one launch (start us, length us, event | category | flops | bytes accessed | tf_op | source)
XLA Modules:
  0.0 60.5 jit_solution(14414486129072715444)
XLA Ops:
  0.6 57.1 %fused.1 = (f32[192,4096]{1,0:T(8,128)S(1)}, f32[96,4096]{1,0:T(8,128)S(1)}) custom-call(f32[192,4096]{1,0:T(8,128)} %bitcast.14, f32[192,4096]{1,0:T(8,128)} %bitcast.15, s32[16,192]{1,0:T(8,128)} %flags_hbm.1), custom_call_target="tpu_custom_call" | custom-call | tf_op jit(solution)/shard_map/fused/pallas_call | solution.py:552
  57.7 1.7 %copy.7 = f32[1,4096,192]{1,2,0:T(8,128)} copy(f32[1,4096,192]{1,2,0:T(8,128)S(1)} %bitcast.12) | data formatting | bytes 6291456
  59.4 1.1 %copy.8 = f32[1,4096,96]{1,2,0:T(8,128)} copy(f32[1,4096,96]{1,2,0:T(8,128)S(1)} %bitcast.13) | data formatting | bytes 3145728

commit v6 on v5

--- a/solution.py
+++ b/solution.py
@@ -18,7 +18,7 @@
 CHUNK = ROWS // CHUNKS
 UNITS = 8
 UNIT = ROWS // UNITS
-FIRST = 3
+FIRST = 4
 EARLY = 6
 RELAYED = 4
 SOURCE = SLICES // 2 - 1

time: 61.2 us -> 61.2 us (level)
  no operation moved by 1% of the time
where the time goes in v6:
time: 61.2 us; the launch traced here: 60.5 us
  Pallas kernels  57.1 us (93%)
  local copies, waits for them, and re-layouts  2.81 us (5%)
  between operations  0.64 us (1%)
    pallas_call x1, Pallas kernels, fused_call(): pl.pallas_call(fused_kernel, out_shape=(shape((W, ROWS), F32), shape((KEE...  57.1 us
    unnamed x2, local copies, waits for them, and re-layouts  2.81 us

profile of v6, /device:TPU:4, one launch (start us, length us, event | category | flops | bytes accessed | tf_op | source)
XLA Modules:
  0.0 60.5 jit_solution(12801058678728211234)
XLA Ops:
  0.6 57.1 %fused.1 = (f32[192,4096]{1,0:T(8,128)S(1)}, f32[96,4096]{1,0:T(8,128)S(1)}) custom-call(f32[192,4096]{1,0:T(8,128)} %bitcast.14, f32[192,4096]{1,0:T(8,128)} %bitcast.15, s32[16,192]{1,0:T(8,128)} %flags_hbm.1), custom_call_target="tpu_custom_call" | custom-call | tf_op jit(solution)/shard_map/fused/pallas_call | solution.py:552
  57.7 1.7 %copy.7 = f32[1,4096,192]{1,2,0:T(8,128)} copy(f32[1,4096,192]{1,2,0:T(8,128)S(1)} %bitcast.12) | data formatting | bytes 6291456
  59.4 1.1 %copy.8 = f32[1,4096,96]{1,2,0:T(8,128)} copy(f32[1,4096,96]{1,2,0:T(8,128)S(1)} %bitcast.13) | data formatting | bytes 3145728
